TPU v7x, 128 devices: a whole 4x4x4 slice. The times are simulated.
128 devices in a mesh: axial: 16 (over z, x), hoop: 8 (over y, core).
Axes of the slice: x: 4, y: 4, z: 4, core: 2. Of those that a mesh axis runs over, the one named last changes fastest.
Arguments:
- start_block: float32 [96, 3, 4, 16, 1024], P(None, None, None, 'axial', 'hoop'), may hold values from -8000 to 8000
- search_block: float32 [96, 3, 4, 16, 1024], P(None, None, None, 'axial', 'hoop'), may hold values from -8000 to 8000
- ritz_values: float32 [96], replicated, may hold values from 2 to 40
- element_matrix: float32 [24, 24], replicated, may hold values from -0.15 to 5, as said below
- moduli: float32 [3], replicated, may hold values from 0.5 to 4
- material_ids: int32 [3, 16, 1024], P(None, 'axial', 'hoop'), may hold values from 0 to 2
- held: int32 [4, 16, 1024], P(None, 'axial', 'hoop'), may hold values 0 or 1
Outputs:
- next_block: float32 [96, 3, 4, 16, 1024], P(None, None, None, 'axial', 'hoop')
- next_search: float32 [96, 3, 4, 16, 1024], P(None, None, None, 'axial', 'hoop')
Inputs may be any that keep to these rules, and one draw needn't show every extreme that they name: `element_matrix`: symmetric; every diagonal entry exceeds the sum of the magnitudes of the other entries of its row.
All inputs are finite; a program needn't handle non-finite values. No bound on the sum of `held` on one device may be relied on, other than what follows from the above.
Results may differ from a plain program's by a relative error of at most 0.0003.
Values sent between devices are 32-bit elements; how exact they have to be, the bound alone decides.
A program may use at most 128 MiB of HBM per device.

v0:
```python
import jax
import jax.numpy as jnp
from jax import lax
from jax.sharding import PartitionSpec as P

CORNERS = [(dr, da, dh) for dr in (0, 1) for da in (0, 1) for dh in (0, 1)]
shift_value = 1.0


def shifted(block, axis, distance):
    devices = range(lax.axis_size(axis))
    route = [((i - distance) % len(devices), i) for i in devices]
    return lax.ppermute(block, axis, route)


def shifted_2(x, axis, by):
    count = lax.axis_size(axis)
    pairs = [(i, i + by) for i in range(count) if 0 <= i + by < count]
    return lax.ppermute(x, axis, pairs)


def corner_products(ext, coef, kmat4, layers, along, beside_all):
    corners = jnp.stack(
        [
            ext[:, :, dr : dr + layers, da : da + along, dh : dh + beside_all]
            for dr, da, dh in CORNERS
        ],
        0,
    )
    parts = jnp.einsum("pqcd,ckdrah->pkqrah", kmat4, corners, precision=lax.Precision.HIGHEST)
    return parts * coef


def assemble(parts, shape, layers, along, beside_all):
    total = jnp.zeros(shape, jnp.float32)
    for index, (dr, da, dh) in enumerate(CORNERS):
        total = total.at[:, :, dr : dr + layers, da : da + along, dh : dh + beside_all].add(
            parts[index]
        )
    return total


def apply_returned(field, coef, kmat4, free):
    layers, along, beside_all = coef.shape
    hoop_next = shifted(field[..., :1], "hoop", -1)
    ext = jnp.concatenate([field, hoop_next], 4)
    axial_next = shifted_2(ext, "axial", -1)
    ext = jnp.concatenate([ext, axial_next], 3)
    parts = corner_products(ext, coef, kmat4, layers, along, beside_all)
    total = assemble(parts, ext.shape, layers, along, beside_all)
    from_below = shifted_2(total[:, :, :, -1:, :], "axial", 1)
    total = total[:, :, :, :-1, :].at[:, :, :, :1, :].add(from_below)
    from_left = shifted(total[..., -1:], "hoop", 1)
    total = total[..., :-1].at[..., :1].add(from_left)
    return total * free


def transposed_dot(left, right):
    return jnp.dot(left, right.T, precision=lax.Precision.HIGHEST)


def on_device(start_block, search_block, ritz_values, element_matrix, moduli, material_ids, held):
    width = start_block.shape[0]
    free = (1 - held).astype(jnp.float32)
    kmat4 = element_matrix.reshape(8, 3, 8, 3)
    coef = jnp.zeros(material_ids.shape, jnp.float32)
    for material in range(moduli.shape[0]):
        coef = coef + jnp.where(material_ids == material, moduli[material], jnp.float32(0.0))
    start_free = start_block * free
    search_free = search_block * free

    def operate(field):
        return apply_returned(field, coef, kmat4, free)

    image_start = operate(start_free)
    image_search = operate(search_free)
    residual = image_start - ritz_values[:, None, None, None, None] * start_free
    image_residual = operate(residual)
    pieces = [
        start_free.reshape(width, -1),
        residual.reshape(width, -1),
        search_free.reshape(width, -1),
    ]
    images = [
        image_start.reshape(width, -1),
        image_residual.reshape(width, -1),
        image_search.reshape(width, -1),
    ]
    basis = jnp.concatenate(pieces, 0)
    stacked = jnp.concatenate(images, 0)
    cross = transposed_dot(basis, stacked)
    inner = transposed_dot(basis, basis)
    cross, inner = lax.psum((cross, inner), ("axial", "hoop"))
    gram_a = 0.5 * (cross + cross.T)
    system = jnp.linalg.cholesky(gram_a + shift_value * inner)
    weights = jax.scipy.linalg.cho_solve((system, True), inner[:, :width])
    keep = (jnp.arange(3 * width) >= width).astype(jnp.float32)[:, None]
    weights_search = weights * keep
    small = jnp.dot(
        weights.T,
        jnp.dot(inner, weights, precision=lax.Precision.HIGHEST),
        precision=lax.Precision.HIGHEST,
    )
    lower = jnp.linalg.cholesky(small)
    rotate = jax.scipy.linalg.solve_triangular(lower, weights.T, lower=True)
    rotate_search = jax.scipy.linalg.solve_triangular(lower, weights_search.T, lower=True)
    unknowns = basis.shape[1] * lax.axis_size("axial") * lax.axis_size("hoop")
    factor = jnp.sqrt(jnp.float32(unknowns))
    both = (
        jnp.dot(jnp.concatenate([rotate, rotate_search], 0), basis, precision=lax.Precision.HIGHEST)
        * factor
    )
    next_block = both[:width].reshape(start_block.shape)
    next_search = both[width:].reshape(start_block.shape)
    return (next_block, next_search)


def solution(mesh):
    in_specs = (
        P(None, None, None, "axial", "hoop"),
        P(None, None, None, "axial", "hoop"),
        P(),
        P(),
        P(),
        P(None, "axial", "hoop"),
        P(None, "axial", "hoop"),
    )
    out_specs = (P(None, None, None, "axial", "hoop"), P(None, None, None, "axial", "hoop"))
    return jax.shard_map(
        on_device, mesh=mesh, in_specs=in_specs, out_specs=out_specs, check_vma=False
    )
```

profile of v0, /device:TPU:1, one launch (start us, length us, event | category | flops | bytes accessed | tf_op | source)
XLA Modules:
  0.0 665.5 jit_solution(2656910727315366129)
XLA Ops:
  20.4 14.4 %collective-permute-done.1 = f32[96,3,4,1,129]{0,2,4,3,1:T(4,128)S(1)} collective-permute-done((f32[96,3,4,1,129]{0,2,4,3,1:T(4,128)}, f32[96,3,4,1,129]{0,2,4,3,1:T(4,128)S(1)}, u32[]{:S(2)}, u32[]{:S(2)}) %collective-permute-start.1) | collective-permute-done | bytes 594464 | tf_op jit(solution)/shard_map/ppermute | solution.py:19
  46.4 7.4 %fusion.8 = f32[8,96,3,3,1,128]{5,0,2,3,1,4:T(8,128)S(1)} fusion(f32[8,3,8,3,1,1]{2,0,3,1,5,4:T(8,128)S(1)} %copy.1944, f32[8,96,3,3,1,128]{5,1,4,3,2,0:T(8,128)} %bitcast_dynamic-update-slice_fusion.17, f32[3,128]{1,0:T(4,128)S(1)} %bitcast.270), kind=kOutput, calls=%fused_computation.13 | convolution fusion | flops 255688704 | bytes 7081728 | tf_op jit(solution)/shard_map/pqcd,ckdrah->pkqrah/dot_general | solution.py:30
  67.5 4.7 scatter-add.95
  75.4 4.7 scatter-add.99
  83.4 4.7 scatter-add.101
  93.4 14.3 %collective-permute-done.2 = f32[96,3,4,1,129]{0,2,4,3,1:T(4,128)S(1)} collective-permute-done((f32[96,3,4,1,129]{0,2,4,3,1:T(4,128)S(1)}, f32[96,3,4,1,129]{0,2,4,3,1:T(4,128)S(1)}, u32[]{:S(2)}, u32[]{:S(2)}) %collective-permute-start.2) | collective-permute-done | bytes 594464 | tf_op jit(solution)/shard_map/ppermute | solution.py:19
  110.0 5.5 collective-permute-start.3
  133.3 16.7 %collective-permute-done.5 = f32[96,3,4,1,129]{0,2,4,3,1:T(4,128)S(1)} collective-permute-done((f32[96,3,4,1,129]{0,2,4,3,1:T(4,128)}, f32[96,3,4,1,129]{0,2,4,3,1:T(4,128)S(1)}, u32[]{:S(2)}, u32[]{:S(2)}) %collective-permute-start.5) | collective-permute-done | bytes 594464 | tf_op jit(solution)/shard_map/ppermute | solution.py:19
  166.7 7.3 %fusion.5 = f32[8,96,3,3,1,128]{5,0,2,3,1,4:T(8,128)S(1)} fusion(f32[8,3,8,3,1,1]{2,0,3,1,5,4:T(8,128)S(1)} %copy-done.16, f32[8,96,3,3,128,1]{4,2,3,1,0,5:T(4,128)} %bitcast.37, f32[3,128]{1,0:T(4,128)S(1)} %bitcast.271), kind=kOutput, calls=%fused_computation.9 | convolution fusion | flops 255688704 | bytes 7081728 | tf_op jit(solution)/shard_map/pqcd,ckdrah->pkqrah/dot_general | solution.py:30
  180.0 4.6 scatter-add.106
  188.8 4.5 scatter-add.110
  196.6 4.7 scatter-add.114
  204.6 4.7 scatter-add.116
  211.1 14.2 %collective-permute-start.6 = (f32[96,3,4,1,129]{0,2,4,3,1:T(4,128)S(1)}, f32[96,3,4,1,129]{0,2,4,3,1:T(4,128)S(1)}, u32[]{:S(2)}, u32[]{:S(2)}) collective-permute-start(f32[96,3,4,1,129]{0,2,4,3,1:T(4,128)S(1)} %copy.1901), channel_id=1, source_target_pairs={{0,8},{8,16},{16,24},{24,32},{32,40},{40,48},{48,56},{56,64},{64,7... | collective-permute-start | bytes 1783304 | tf_op jit(solution)/shard_map/ppermute | solution.py:19
  225.3 6.7 %collective-permute-done.6 = f32[96,3,4,1,129]{0,2,4,3,1:T(4,128)S(1)} collective-permute-done((f32[96,3,4,1,129]{0,2,4,3,1:T(4,128)S(1)}, f32[96,3,4,1,129]{0,2,4,3,1:T(4,128)S(1)}, u32[]{:S(2)}, u32[]{:S(2)}) %collective-permute-start.6) | collective-permute-done | bytes 594464 | tf_op jit(solution)/shard_map/ppermute | solution.py:19
  257.0 16.5 %collective-permute-done.9 = f32[96,3,4,1,129]{0,2,4,3,1:T(4,128)S(1)} collective-permute-done((f32[96,3,4,1,129]{0,2,4,3,1:T(4,128)}, f32[96,3,4,1,129]{0,2,4,3,1:T(4,128)S(1)}, u32[]{:S(2)}, u32[]{:S(2)}) %collective-permute-start.9) | collective-permute-done | bytes 594464 | tf_op jit(solution)/shard_map/ppermute | solution.py:19
  291.9 7.3 %fusion.2 = f32[8,96,3,3,1,128]{5,0,2,3,1,4:T(8,128)S(1)} fusion(f32[8,3,8,3,1,1]{2,0,3,1,5,4:T(8,128)S(1)} %copy-done.17, f32[8,96,3,3,128,1]{4,2,3,1,0,5:T(4,128)} %bitcast.60, f32[3,128]{1,0:T(4,128)S(1)} %bitcast.272), kind=kOutput, calls=%fused_computation.5 | convolution fusion | flops 255688704 | bytes 7081728 | tf_op jit(solution)/shard_map/pqcd,ckdrah->pkqrah/dot_general | solution.py:30
  314.0 4.5 scatter-add.125
  322.8 4.5 scatter-add.129
  331.5 4.5 scatter-add.131
  341.0 7.2 %collective-permute-start.10 = (f32[96,3,4,1,129]{0,2,4,3,1:T(4,128)}, f32[96,3,4,1,129]{0,2,4,3,1:T(4,128)}, u32[]{:S(2)}, u32[]{:S(2)}) collective-permute-start(f32[96,3,4,1,129]{0,2,4,3,1:T(4,128)} %copy.1928), channel_id=1, source_target_pairs={{0,8},{8,16},{16,24},{24,32},{32,40},{40,48},{48,56},{56,64},{64,7... | collective-permute-start | bytes 1783304 | tf_op jit(solution)/shard_map/ppermute | solution.py:19
  352.1 11.2 %collective-permute-done.10 = f32[96,3,4,1,129]{0,2,4,3,1:T(4,128)} collective-permute-done((f32[96,3,4,1,129]{0,2,4,3,1:T(4,128)}, f32[96,3,4,1,129]{0,2,4,3,1:T(4,128)}, u32[]{:S(2)}, u32[]{:S(2)}) %collective-permute-start.10) | collective-permute-done | bytes 594464 | tf_op jit(solution)/shard_map/ppermute | solution.py:19
  385.8 4.7 fusion.16
  391.2 151.2 %all-reduce.9.cloned.1.call-done = (f32[288,288]{1,0:T(8,128)}, f32[288,288]{0,1:T(8,128)}) async-done(((f32[288,288]{1,0:T(8,128)}, f32[288,288]{0,1:T(8,128)}), (f32[288,288]{1,0:T(8,128)}, f32[288,288]{0,1:T(8,128)})) %all-reduce.9.cloned.1.call-update) | async-done | bytes 663568 | tf_op jit(solution)/shard_map/psum | solution.py:93
  545.1 11.7 %cholesky.94 = f32[128,128]{1,0:T(8,128)S(1)} custom-call(f32[128,128]{1,0:T(8,128)S(1)} %cholesky.236), custom_call_target="Cholesky" | custom-call | tf_op jit(solution)/shard_map/jit(cholesky)/cholesky | solution.py:95
  556.9 9.8 %custom-call.32 = f32[1,128,128]{1,2,0:T(8,128)S(1)} custom-call(f32[1,128,128]{2,1,0:T(8,128)S(1)} %get-tuple-element.531), custom_call_target="InvertDiagBlocksLowerTriangular" | custom-call | tf_op jit(solution)/shard_map/jit(cholesky)/cholesky | solution.py:95
  567.3 11.9 %cholesky.193 = f32[128,128]{1,0:T(8,128)S(1)} custom-call(f32[128,128]{1,0:T(8,128)S(1)} %cholesky.240), custom_call_target="Cholesky" | custom-call | tf_op jit(solution)/shard_map/jit(cholesky)/cholesky | solution.py:95
  579.1 9.8 %custom-call.33 = f32[1,128,128]{1,2,0:T(8,128)S(1)} custom-call(f32[1,128,128]{2,1,0:T(8,128)S(1)} %get-tuple-element.528), custom_call_target="InvertDiagBlocksLowerTriangular" | custom-call | tf_op jit(solution)/shard_map/jit(cholesky)/cholesky | solution.py:95
  595.8 5.2 while.34
  602.9 29.7 %custom-call.34 = f32[3,128,128]{1,2,0:T(8,128)S(1)} custom-call(f32[3,128,128]{2,1,0:T(8,128)S(1)} %pad_maximum_fusion.3), custom_call_target="InvertDiagBlocksLowerTriangular" | custom-call | tf_op jit(solution)/shard_map/jit(_cho_solve)/triangular_solve | solution.py:96
  636.0 8.8 %cholesky.227 = f32[96,96]{1,0:T(8,128)S(1)} custom-call(f32[96,96]{1,0:T(8,128)S(1)} %fusion.80), custom_call_target="Cholesky" | custom-call | tf_op jit(solution)/shard_map/jit(cholesky)/cholesky | solution.py:104
  646.1 7.4 %custom-call.36 = f32[1,96,96]{1,2,0:T(8,128)S(1)} custom-call(f32[1,96,96]{2,1,0:T(8,128)S(1)} %fusion.77), custom_call_target="InvertDiagBlocksLowerTriangular" | custom-call | tf_op jit(solution)/shard_map/jit(_solve_triangular)/triangular_solve | solution.py:105
  (260 shorter events, 228.7 us)
Async XLA Ops:
  7.2 535.3 %all-reduce.9.cloned.1.call-start = ((), (), s32[]{:S(2)}) async-start(), calls=%async_computation | async-start | bytes 1769472 | tf_op jit(solution)/shard_map/psum | solution.py:93
  9.2 4.0 collective-permute-start
  12.1 4.2 copy-start.20
  12.1 6.1 copy-start.19
  14.9 19.9 %collective-permute-start.1 = (f32[96,3,4,1,129]{0,2,4,3,1:T(4,128)}, f32[96,3,4,1,129]{0,2,4,3,1:T(4,128)S(1)}, u32[]{:S(2)}, u32[]{:S(2)}) collective-permute-start(f32[96,3,4,1,129]{0,2,4,3,1:T(4,128)} %copy.1856), channel_id=1, source_target_pairs={{8,0},{16,8},{24,16},{32,24},{40,32},{48,40},{56,48},{64,56},{72,6... | collective-permute-start | bytes 1783304 | tf_op jit(solution)/shard_map/ppermute | solution.py:19
  18.5 27.9 %copy-start.15 = (f32[8,3,8,3,1,1]{2,0,3,1,5,4:T(8,128)}, f32[8,3,8,3,1,1]{2,0,3,1,5,4:T(8,128)S(1)}, u32[]{:S(2)}) copy-start(f32[8,3,8,3,1,1]{2,0,3,1,5,4:T(8,128)S(1)} %copy.1944) | copy-start | bytes 6916
  39.8 4.5 copy-start
  58.0 8.2 %copy-start.11 = (f32[1,96,3,3,1,128]{5,0,2,3,1,4:T(1,128)S(1)}, f32[1,96,3,3,1,128]{5,0,2,3,1,4:T(1,128)}, u32[]{:S(2)}) copy-start(f32[1,96,3,3,1,128]{5,0,2,3,1,4:T(1,128)} %get-tuple-element.495) | copy-start | bytes 1327108
  90.0 17.8 %collective-permute-start.2 = (f32[96,3,4,1,129]{0,2,4,3,1:T(4,128)S(1)}, f32[96,3,4,1,129]{0,2,4,3,1:T(4,128)S(1)}, u32[]{:S(2)}, u32[]{:S(2)}) collective-permute-start(f32[96,3,4,1,129]{0,2,4,3,1:T(4,128)S(1)} %copy.1871), channel_id=1, source_target_pairs={{0,8},{8,16},{16,24},{24,32},{32,40},{40,48},{48,56},{56,64},{64,7... | collective-permute-start | bytes 1783304 | tf_op jit(solution)/shard_map/ppermute | solution.py:19
  109.8 11.2 %copy-start.3 = (f32[96,3,4,1,128]{4,3,2,1,0:T(1,128)S(1)}, f32[96,3,4,1,128]{4,3,2,1,0:T(1,128)}, u32[]{:S(2)}) copy-start(f32[96,3,4,1,128]{4,3,2,1,0:T(1,128)} %param.75) | copy-start | bytes 1769476
  110.0 6.2 collective-permute-start.3
  122.8 3.7 collective-permute-start.4
  128.3 21.7 %collective-permute-start.5 = (f32[96,3,4,1,129]{0,2,4,3,1:T(4,128)}, f32[96,3,4,1,129]{0,2,4,3,1:T(4,128)S(1)}, u32[]{:S(2)}, u32[]{:S(2)}) collective-permute-start(f32[96,3,4,1,129]{0,2,4,3,1:T(4,128)} %copy.1884), channel_id=1, source_target_pairs={{8,0},{16,8},{24,16},{32,24},{40,32},{48,40},{56,48},{64,56},{72,6... | collective-permute-start | bytes 1783304 | tf_op jit(solution)/shard_map/ppermute | solution.py:19
  151.6 4.5 copy-start.1
  157.5 6.2 copy-start.12
  157.5 7.4 %copy-start.6 = (f32[96,3,3,1,128]{4,1,2,0,3:T(4,128)S(1)}, f32[96,3,3,1,128]{4,1,2,0,3:T(4,128)}, u32[]{:S(2)}) copy-start(f32[96,3,3,1,128]{4,1,2,0,3:T(4,128)} %copy.1889) | copy-start | bytes 1327108
  161.6 5.1 copy-start.16
  179.9 13.4 %copy-start.10 = (f32[1,96,3,3,1,128]{5,0,2,3,1,4:T(1,128)S(1)}, f32[1,96,3,3,1,128]{5,0,2,3,1,4:T(1,128)}, u32[]{:S(2)}) copy-start(f32[1,96,3,3,1,128]{5,0,2,3,1,4:T(1,128)} %get-tuple-element.478) | copy-start | bytes 1327108
  184.5 10.7 %copy-start.9 = (f32[1,96,3,3,1,128]{5,0,2,3,1,4:T(1,128)S(1)}, f32[1,96,3,3,1,128]{5,0,2,3,1,4:T(1,128)}, u32[]{:S(2)}) copy-start(f32[1,96,3,3,1,128]{5,0,2,3,1,4:T(1,128)} %get-tuple-element.477) | copy-start | bytes 1327108
  211.1 20.9 %collective-permute-start.6 = (f32[96,3,4,1,129]{0,2,4,3,1:T(4,128)S(1)}, f32[96,3,4,1,129]{0,2,4,3,1:T(4,128)S(1)}, u32[]{:S(2)}, u32[]{:S(2)}) collective-permute-start(f32[96,3,4,1,129]{0,2,4,3,1:T(4,128)S(1)} %copy.1901), channel_id=1, source_target_pairs={{0,8},{8,16},{16,24},{24,32},{32,40},{40,48},{48,56},{56,64},{64,7... | collective-permute-start | bytes 1783304 | tf_op jit(solution)/shard_map/ppermute | solution.py:19
  235.2 3.4 collective-permute-start.7
  238.3 3.6 copy-start.18
  244.7 3.3 collective-permute-start.8
  252.0 21.5 %collective-permute-start.9 = (f32[96,3,4,1,129]{0,2,4,3,1:T(4,128)}, f32[96,3,4,1,129]{0,2,4,3,1:T(4,128)S(1)}, u32[]{:S(2)}, u32[]{:S(2)}) collective-permute-start(f32[96,3,4,1,129]{0,2,4,3,1:T(4,128)} %copy.1911), channel_id=1, source_target_pairs={{8,0},{16,8},{24,16},{32,24},{40,32},{48,40},{56,48},{64,56},{72,6... | collective-permute-start | bytes 1783304 | tf_op jit(solution)/shard_map/ppermute | solution.py:19
  283.6 4.1 copy-start.14
  283.6 5.3 copy-start.13
  285.7 5.2 copy-start.7
  287.8 4.1 copy-start.17
  341.0 22.3 %collective-permute-start.10 = (f32[96,3,4,1,129]{0,2,4,3,1:T(4,128)}, f32[96,3,4,1,129]{0,2,4,3,1:T(4,128)}, u32[]{:S(2)}, u32[]{:S(2)}) collective-permute-start(f32[96,3,4,1,129]{0,2,4,3,1:T(4,128)} %copy.1928), channel_id=1, source_target_pairs={{0,8},{8,16},{16,24},{24,32},{32,40},{40,48},{48,56},{56,64},{64,7... | collective-permute-start | bytes 1783304 | tf_op jit(solution)/shard_map/ppermute | solution.py:19
  369.0 10.1 %collective-permute-start.11 = (f32[96,3,4,1,1]{0,2,4,3,1:T(4,128)S(1)}, f32[96,3,4,1,1]{0,2,4,3,1:T(4,128)}, u32[]{:S(2)}, u32[]{:S(2)}) collective-permute-start(f32[96,3,4,1,1]{0,2,4,3,1:T(4,128)S(1)} %copy.1930), channel_id=1, source_target_pairs={{7,0},{0,1},{1,2},{2,3},{3,4},{4,5},{5,6},{6,7},{15,8},{8,9},{9,10... | collective-permute-start | bytes 13832 | tf_op jit(solution)/shard_map/ppermute | solution.py:13
  380.0 5.7 copy-start.4
  545.1 87.4 %copy-start.2 = (f32[288,288]{1,0:T(8,128)S(1)}, f32[288,288]{1,0:T(8,128)}, u32[]{:S(2)}) copy-start(f32[288,288]{1,0:T(8,128)} %get-tuple-element.469) | copy-start | bytes 995332
  (2 other events, 2.6 us)
Sparse Core Ops, SparseCore 0:
  390.7 151.7 all-reduce.8
where the time goes:
time: 678 us; the launch traced here: 665 us
  waiting for transfers between devices  236 us (35%)
  local copies, waits for them, and re-layouts  176 us (26%)
  other arithmetic  155 us (23%)
  starting transfers between devices  44 us (6%)
  matrix products  37.1 us (5%)
  between operations  17.1 us (3%)
    psum x1, waiting for transfers between devices, on_device(): cross, inner = lax.psum((cross, inner), ('axial', 'hoop'))  151 us
    ppermute x6, waiting for transfers between devices, shifted_2(): return lax.ppermute(x, axis, pairs)  79.9 us
    scatter-add x15, local copies, waits for them, and re-layouts, assemble(): total.at[:, :, dr:dr + layers, da:da + along, dh:dh + beside_all]  60.1 us
    another operation x10, other arithmetic, on_device(): system = jnp.linalg.cholesky(gram_a + shift_value * inner)  47.6 us
    another operation x7, other arithmetic, on_device(): weights = jax.scipy.linalg.cho_solve((system, True), inner[:, :width])  32.2 us
    unnamed x68, local copies, waits for them, and re-layouts  29.2 us
    ppermute x6, starting transfers between devices, shifted_2(): return lax.ppermute(x, axis, pairs)  28.7 us
    dot_general x3, matrix products, corner_products(): jnp.einsum('pqcd,ckdrah->pkqrah', kmat4, corners, precision=lax.Precision...  21.9 us
  transfers between devices with their start and end apart: 13, of which 11 were waited for; matrix products, arithmetic and copies ran while one was open for 4% of the time, Pallas kernels for 0%

commit v1 on v0

v1 whole, which is shorter than its diff:
```python
import functools
import math

import jax
import jax.numpy as jnp
from jax import lax
from jax.experimental import pallas as pl
from jax.experimental.pallas import tpu as pltpu
from jax.sharding import PartitionSpec as P

HI = lax.Precision.HIGHEST
MESH = pl.DeviceIdType.MESH
K = 96
F32 = jnp.float32
BF16 = jnp.bfloat16
VMEM = pl.BlockSpec(memory_space=pltpu.VMEM)
SMEM = pl.BlockSpec(memory_space=pltpu.SMEM)
ROOM = 48 * 2**20
UNKNOWNS = 196608


def mm(a, b):
    return lax.dot_general(a, b, (((1,), (0,)), ((), ())), precision=HI, preferred_element_type=jnp.float32)

def mm_t(a, b):
    return lax.dot_general(a, b, (((0,), (0,)), ((), ())), precision=HI, preferred_element_type=jnp.float32)


def sweep(block, factor):
    lane = lax.broadcasted_iota(jnp.int32, (8, 128), 1)
    sub = lax.broadcasted_iota(jnp.int32, (8, 128), 0)
    tiles = [block[8 * t : 8 * t + 8, :] for t in range(12)]
    found = []
    for group in range(24):
        p = 4 * group
        home, low = p // 8, p % 8
        cols = [[jnp.broadcast_to(tile[:, p + j : p + j + 1], (8, 128)) for tile in tiles] for j in range(4)]
        rows = [jnp.broadcast_to(tiles[home][low + j : low + j + 1, :], (8, 128)) for j in range(4)]

        def entry(i, j):
            return jnp.broadcast_to(cols[j][home][low + i : low + i + 1, :], (8, 128))

        a00, a01, a11 = entry(0, 0), entry(0, 1), entry(1, 1)
        b00, b01, b10, b11 = entry(0, 2), entry(0, 3), entry(1, 2), entry(1, 3)
        c00, c01, c11 = entry(2, 2), entry(2, 3), entry(3, 3)
        ia = 1.0 / (a00 * a11 - a01 * a01)
        h00, h01, h11 = a11 * ia, -a01 * ia, a00 * ia
        x00, x01 = h00 * b00 + h01 * b10, h00 * b01 + h01 * b11
        x10, x11 = h01 * b00 + h11 * b10, h01 * b01 + h11 * b11
        s00 = c00 - (b00 * x00 + b10 * x10)
        s01 = c01 - (b00 * x01 + b10 * x11)
        s11 = c11 - (b01 * x01 + b11 * x11)
        ic = 1.0 / (s00 * s11 - s01 * s01)
        g00, g01, g11 = s11 * ic, -s01 * ic, s00 * ic
        picked = (lane >= p) & (lane < p + 4)
        full = [jnp.where(picked, jnp.where(lane == p + j, 1.0, 0.0), rows[j]) for j in range(4)]
        u0 = full[2] - (x00 * full[0] + x10 * full[1])
        u1 = full[3] - (x01 * full[0] + x11 * full[1])
        n2 = g00 * u0 + g01 * u1
        n3 = g01 * u0 + g11 * u1
        v0 = h00 * full[0] + h01 * full[1]
        v1 = h01 * full[0] + h11 * full[1]
        n0 = v0 - (x00 * n2 + x01 * n3)
        n1 = v1 - (x10 * n2 + x11 * n3)
        new = [n0, n1, n2, n3]
        if factor:
            left = [jnp.where(lane < p + 4, f, 0.0) for f in full]
            w0 = lax.rsqrt(a00)
            l0 = left[0] * w0
            e1 = a11 - a01 * a01 / a00
            l1 = (left[1] - (a01 / a00) * left[0]) * lax.rsqrt(e1)
            y0 = jnp.where(lane < p + 4, u0, 0.0)
            y1 = jnp.where(lane < p + 4, u1, 0.0)
            l2 = y0 * lax.rsqrt(s00)
            l3 = (y1 - (s01 / s00) * y0) * lax.rsqrt(s11 - s01 * s01 / s00)
            found.append([l0, l1, l2, l3])
        fresh = []
        for t, tile in enumerate(tiles):
            kept = jnp.where(picked, 0.0, tile)
            if t == home:
                here = (sub >= low) & (sub < low + 4)
                kept = jnp.where(here, 0.0, kept)
                q = [jnp.where(here, jnp.where(sub == low + j, -1.0, 0.0), cols[j][t]) for j in range(4)]
            else:
                q = [cols[j][t] for j in range(4)]
            fresh.append(kept - ((q[0] * n0 + q[1] * n1) + (q[2] * n2 + q[3] * n3)))
        tiles = fresh
    if factor:
        out = []
        for t in range(12):
            eight = found[2 * t] + found[2 * t + 1]
            tile = eight[0]
            for s in range(1, 8):
                tile = jnp.where(sub == s, eight[s], tile)
            out.append(tile)
        return jnp.concatenate(out, 0)
    return jnp.concatenate(tiles, 0)


def diagonal(block):
    lane = lax.broadcasted_iota(jnp.int32, (K, 128), 1)
    row = lax.broadcasted_iota(jnp.int32, (K, 128), 0)
    only = jnp.where(lane == row, block, 0.0)
    down = jnp.sum(only, 1, keepdims=True)
    along = jnp.sum(only, 0, keepdims=True)
    return lax.rsqrt(down), lax.rsqrt(jnp.where(along == 0.0, 1.0, along))


def cut(block):
    return block[:, :K]


def pad(block):
    return jnp.concatenate([block, jnp.zeros((block.shape[0], 128 - block.shape[1]), jnp.float32)], 1)


def rotation(gram, scale, rot_ref):
    b = [gram[i] for i in range(6)]
    a = [gram[6 + i] for i in range(6)]
    m = [x + y for x, y in zip(a, b)]
    d0, e0 = diagonal(m[0])
    d1, e1 = diagonal(m[3])
    d2, e2 = diagonal(m[5])
    m11, m12, m13 = m[0] * d0 * e0, m[1] * d0 * e1, m[2] * d0 * e2
    m22, m23, m33 = m[3] * d1 * e1, m[4] * d1 * e2, m[5] * d2 * e2
    bsr_t, bsp_t, brp_t = (pad(cut(x).T) for x in (b[1], b[2], b[4]))
    f1, f2, f3 = b[0] * d0, bsr_t * d1, bsp_t * d2
    i1 = sweep(m11, False)
    t1 = mm(cut(i1), jnp.concatenate([m12, m13, f1], 1))
    t12, t13, y1 = t1[:, :128], t1[:, 128:256], t1[:, 256:]
    s2 = jnp.concatenate([m22, m23, f2], 1) - mm(cut(m12).T, t1)
    s3 = jnp.concatenate([m33, f3], 1) - mm(cut(m13).T, t1[:, 128:])
    i2 = sweep(s2[:, :128], False)
    m23 = s2[:, 128:256]
    t2 = mm(cut(i2), s2[:, 128:])
    s3 = s3 - mm(cut(m23).T, t2)
    i3 = sweep(s3[:, :128], False)
    w3 = mm(cut(i3), s3[:, 128:])
    w2 = t2[:, 128:] - mm(cut(t2), w3)
    w1 = y1 - mm(jnp.concatenate([cut(t12), cut(t13)], 1), jnp.concatenate([w2, w3], 0))
    w = jnp.concatenate([w1 * d0, w2 * d1, w3 * d2], 0)
    big = jnp.concatenate(
        [
            jnp.concatenate([cut(b[0]), cut(b[1]), cut(b[2])], 1),
            jnp.concatenate([cut(bsr_t), cut(b[3]), cut(b[4])], 1),
            jnp.concatenate([cut(bsp_t), cut(brp_t), cut(b[5])], 1),
        ],
        0,
    )
    wt = cut(w).T
    small = mm(wt, mm(big, w))
    ds, es = diagonal(small)
    inv = sweep(small * ds * es, True) * es
    rot_ref[...] = mm(cut(inv), wt) * scale


def mm_nt(a, b):
    return lax.dot_general(a, b, (((1,), (1,)), ((), ())), precision=HI, preferred_element_type=F32)


def call(kernel, shapes, count, scratch=(), memory=None, name=None):
    return pl.pallas_call(
        kernel,
        out_shape=[jax.ShapeDtypeStruct(*shape) for shape in shapes],
        in_specs=memory or [VMEM] * count,
        out_specs=[VMEM] * len(shapes),
        scratch_shapes=list(scratch),
        compiler_params=pltpu.CompilerParams(vmem_limit_bytes=ROOM),
        name=name,
    )


def split(x):
    high = x.astype(BF16)
    rest = x - high.astype(F32)
    middle = rest.astype(BF16)
    low = (rest - middle.astype(F32)).astype(BF16)
    return high, middle, low


def stencil(kmat):
    def rows_of(shape, axis):
        at = lax.broadcasted_iota(jnp.int32, shape, axis)
        low, high = at % 8, at // 8
        dh, high = high % 2, high // 2
        return low // 3, low % 3, dh, high % 3, high // 3, low < 6

    def columns_of(shape, axis):
        at = lax.broadcasted_iota(jnp.int32, shape, axis)
        low, high = at % 8, at // 8
        return low // 3, low % 3, high // 4, high % 4, low < 6

    da, q, dh, _, dr, real = rows_of((96, 24), 0)
    corner = lax.broadcasted_iota(jnp.int32, (96, 24), 1)
    pick = jnp.where(real & (corner == 3 * (4 * dr + 2 * da + dh) + q), 1.0, 0.0)
    picked = mm(pick, kmat)
    layer = rows_of((96, 64), 0)[3]
    node = columns_of((96, 64), 1)[3]
    total = jnp.zeros((96, 64), F32)
    for dr in range(2):
        da, q, dh, _, real = columns_of((24, 64), 1)
        corner = lax.broadcasted_iota(jnp.int32, (24, 64), 0)
        place = jnp.where(real & (corner == 3 * (4 * dr + 2 * da + dh) + q), 1.0, 0.0)
        total = total + jnp.where(node == layer + dr, mm(picked, place), 0.0)
    high, middle, low = split(total)
    return jnp.concatenate([high, high, high, middle, middle, low], 1)


def put(field_ref, near, far, near_edge, far_edge):
    lane = lax.broadcasted_iota(jnp.int32, (K, 128), 1)
    zero = jnp.zeros((K, 128), F32)
    for high in range(8):
        for low in (6, 7):
            field_ref[pl.ds(8 * high + low, K, stride=64), :] = zero
    for da, (field, edge) in enumerate(((near, near_edge), (far, far_edge))):
        edge = edge[...]
        for q in range(3):
            for r in range(4):
                i = 4 * q + r
                tile = field[:, 128 * i : 128 * i + 128]
                field_ref[pl.ds(8 * r + 3 * da + q, K, stride=64), :] = tile
                moved = jnp.where(lane == 127, pltpu.roll(edge, 127 - i, 1), pltpu.roll(tile, 127, 1))
                field_ref[pl.ds(32 + 8 * r + 3 * da + q, K, stride=64), :] = moved


def products(field_ref, image_ref, stencil_ref, coef):
    weights = stencil_ref[...]
    coef = [jnp.broadcast_to(coef[r : r + 1], (8, 128)) for r in range(3)]

    def step(pair, carry):
        base = pl.multiple_of(128 * pair, 128)
        both = field_ref[pl.ds(base, 128), :]
        high, middle, low = split(jnp.concatenate([both[:64], both[64:]], 1))
        stack = jnp.concatenate([high, middle, low, high, middle, high], 0)
        terms = jnp.dot(weights, stack, preferred_element_type=F32)
        for half in range(2):
            term = terms[:, 128 * half : 128 * half + 128]

            def part(dr, r, dh):
                at = 8 * ((dr * 3 + r) * 2 + dh)
                return term[at : at + 8] * coef[r]

            for dh in range(2):
                for node in range(4):
                    parts = [part(dr, node - dr, dh) for dr in range(2) if 0 <= node - dr < 3]
                    value = parts[0] if len(parts) == 1 else parts[0] + parts[1]
                    image_ref[pl.ds(base + 64 * half + 32 * dh + 8 * node, 8), :] = value
        return carry

    lax.fori_loop(0, K // 2, step, 0, unroll=2)


def take(image_ref, da, store):
    lane = lax.broadcasted_iota(jnp.int32, (K, 128), 1)
    over = jnp.zeros((K, 128), F32)
    for q in range(3):
        for r in range(4):
            i = 4 * q + r
            at = 8 * r + 3 * da + q
            first = image_ref[pl.ds(at, K, stride=64), :]
            second = pltpu.roll(image_ref[pl.ds(32 + at, K, stride=64), :], 1, 1)
            store(i, first + jnp.where(lane == 0, 0.0, second))
            over = jnp.where(lane == i, pltpu.roll(second, i, 1), over)
    return over


def coefficients(ids_ref, moduli_ref):
    ids = ids_ref[...]
    coef = jnp.zeros(ids.shape, F32)
    for material in range(3):
        coef = coef + jnp.where(ids == material, moduli_ref[material], 0.0)
    return coef


def load_kernel(start_ref, search_ref, held_ref, kmat_ref, s_ref, p_ref, s_edge_ref, p_edge_ref, stencil_ref):
    free = (1 - held_ref[...]).astype(F32)
    lane = lax.broadcasted_iota(jnp.int32, (K, 128), 1)
    for source, field, edge_ref in ((start_ref, s_ref, s_edge_ref), (search_ref, p_ref, p_edge_ref)):
        edge = jnp.zeros((K, 128), F32)
        for i in range(12):
            tile = source[pl.ds(i, K, stride=12), :] * free[i % 4 : i % 4 + 1]
            field[:, 128 * i : 128 * i + 128] = tile
            edge = jnp.where(lane == i, pltpu.roll(tile, i, 1) if i else tile, edge)
        edge_ref[...] = edge
    stencil_ref[...] = stencil(kmat_ref[...])


def image_kernel(
    s_ref, far_ref, edge_ref, far_edge_ref, ids_ref, stencil_ref, moduli_ref,
    near_ref, next_ref, over_ref, next_over_ref, field, image,
):
    put(field, s_ref, far_ref, edge_ref, far_edge_ref)
    products(field, image, stencil_ref, coefficients(ids_ref, moduli_ref))
    for da, (target, over) in enumerate(((near_ref, over_ref), (next_ref, next_over_ref))):

        def store(i, value, target=target):
            target[:, 128 * i : 128 * i + 128] = value

        over[...] = take(image, da, store)


def residual_kernel(s_ref, near_ref, below_ref, over_ref, below_over_ref, held_ref, ritz_ref, image_ref, r_ref, edge_ref):
    free = (1 - held_ref[...]).astype(F32)
    lane = lax.broadcasted_iota(jnp.int32, (K, 128), 1)
    over = over_ref[...] + below_over_ref[...]
    edge = jnp.zeros((K, 128), F32)
    for i in range(12):
        lanes = slice(128 * i, 128 * i + 128)
        came = jnp.where(lane == 0, pltpu.roll(over, 128 - i, 1) if i else over, 0.0)
        image = (near_ref[:, lanes] + below_ref[:, lanes] + came) * free[i % 4 : i % 4 + 1]
        tile = image - ritz_ref[...] * s_ref[:, lanes]
        image_ref[:, lanes] = image
        r_ref[:, lanes] = tile
        edge = jnp.where(lane == i, pltpu.roll(tile, i, 1) if i else tile, edge)
    edge_ref[...] = edge


def gram_kernel(
    s_ref, image_ref, r_ref, r_far_ref, r_edge_ref, r_far_edge_ref, p_ref, p_far_ref, p_edge_ref, p_far_edge_ref,
    ids_ref, stencil_ref, moduli_ref, gram_ref, field, image, wide,
):
    coef = coefficients(ids_ref, moduli_ref)
    blocks = [None] * 12
    s, r, p = s_ref[...], r_ref[...], p_ref[...]
    rows = jnp.concatenate([s, r, p], 0)
    b_s, b_r, b_p = mm_nt(s, rows), mm_nt(r, rows[K:]), mm_nt(p, p)
    a_s = mm_nt(image_ref[...], rows)
    wholes = []
    for near, far, edge, far_edge in (
        (r_ref, r_far_ref, r_edge_ref, r_far_edge_ref),
        (p_ref, p_far_ref, p_edge_ref, p_far_edge_ref),
    ):
        wholes.append(jnp.concatenate([near[...], far[...], edge[...], far_edge[...]], 1))
        put(field, near, far, edge, far_edge)
        products(field, image, stencil_ref, coef)
        for da in range(2):

            def store(i, value, da=da):
                wide[:, 1536 * da + 128 * i : 1536 * da + 128 * i + 128] = value

            wide[:, 3072 + 128 * da : 3200 + 128 * da] = take(image, da, store)
        if len(wholes) == 1:
            a_r_r = mm_nt(wide[...], wholes[0])
            whole = jnp.concatenate([p_ref[...], p_far_ref[...], p_edge_ref[...], p_far_edge_ref[...]], 1)
            a_r_p = mm_nt(wide[...], whole)
        else:
            a_p_p = mm_nt(wide[...], wholes[1])
    blocks = [b_s[:, :K], b_s[:, K : 2 * K], b_s[:, 2 * K :], b_r[:, :K], b_r[:, K:], b_p]
    blocks += [a_s[:, :K], a_s[:, K : 2 * K], a_s[:, 2 * K :], a_r_r, a_r_p, a_p_p]
    blocks = [pad(block) for block in blocks]
    lane = lax.broadcasted_iota(jnp.int32, (K, 128), 1)
    for group in range(3):
        for j in range(3):
            extra = pltpu.roll(blocks[9 + group], 96 - 32 * j, 1)
            whole = jnp.where(lane < K, blocks[3 * group + j], extra)
            gram_ref[12 * (3 * group + j) : 12 * (3 * group + j) + 12] = whole.reshape(12, 8, 128)
    gram_ref[108:128] = jnp.zeros((20, 8, 128), F32)


def unpack(gram_ref):
    lane = lax.broadcasted_iota(jnp.int32, (K, 128), 1)
    blocks = [None] * 12
    for group in range(3):
        extra = jnp.zeros((K, 128), F32)
        for j in range(3):
            whole = gram_ref[12 * (3 * group + j) : 12 * (3 * group + j) + 12].reshape(K, 128)
            blocks[3 * group + j] = jnp.where(lane < K, whole, 0.0)
            here = (lane >= 32 * j) & (lane < 32 * j + 32)
            extra = jnp.where(here, pltpu.roll(whole, 32 + 32 * j, 1), extra)
        blocks[9 + group] = extra
    return blocks


def sum_kernel(g_ref, out_ref, from_core, half, from_x, quarter, from_y, from_z, send, recv):
    axial, hoop = lax.axis_index("axial"), lax.axis_index("hoop")
    z, x = axial // 4, axial % 4
    y, core = hoop // 2, hoop % 2

    def at(z, x, y, core):
        return (z * 4 + x, y * 2 + core)

    def others(axis):
        if axis == "core":
            return [at(z, x, y, 1 - core)]
        turn = [lambda v, d: (v + d) % 4]
        if axis == "x":
            return [at(z, (x + d) % 4, y, core) for d in (1, 2, 3)]
        if axis == "y":
            return [at(z, x, (y + d) % 4, core) for d in (1, 2, 3)]
        return [at((z + d) % 4, x, y, core) for d in (1, 2, 3)]

    barrier = pltpu.get_barrier_semaphore()
    for axis in ("core", "x", "y", "z"):
        for peer in others(axis):
            pl.semaphore_signal(barrier, inc=1, device_id=peer, device_id_type=MESH)
    pl.semaphore_wait(barrier, 10)
    used = [0]

    def copy(source, target, peer):
        index = used[0]
        used[0] += 1
        made = pltpu.make_async_remote_copy(
            src_ref=source, dst_ref=target, send_sem=send.at[index], recv_sem=recv.at[index],
            device_id=peer, device_id_type=MESH,
        )
        made.start()
        return made

    def finish(copies):
        for made in copies:
            made.wait()

    finish([copy(g_ref.at[pl.ds((1 - core) * 64, 64)], from_core, others("core")[0])])
    half[...] = g_ref[pl.ds(core * 64, 64)] + from_core[...]
    finish(
        [
            copy(half.at[pl.ds(((x + d) % 4) * 16, 16)], from_x.at[d - 1], others("x")[d - 1])
            for d in (1, 2, 3)
        ]
    )
    quarter[...] = (half[pl.ds(x * 16, 16)] + from_x[0]) + (from_x[1] + from_x[2])
    finish(
        [
            copy(quarter.at[pl.ds(((y + d) % 4) * 4, 4)], from_y.at[d - 1], others("y")[d - 1])
            for d in (1, 2, 3)
        ]
    )
    from_z[z] = (quarter[pl.ds(y * 4, 4)] + from_y[0]) + (from_y[1] + from_y[2])
    finish([copy(from_z.at[z], from_z.at[z], peer) for peer in others("z")])
    base = core * 64 + x * 16 + y * 4
    out_ref[pl.ds(base, 4)] = (from_z[0] + from_z[1]) + (from_z[2] + from_z[3])
    for axis, first, size in (("y", base, 4), ("x", core * 64 + x * 16, 16), ("core", core * 64, 64)):
        part = out_ref.at[pl.ds(first, size)]
        finish([copy(part, part, peer) for peer in others(axis)])


def sum_over_devices(gram):
    def tiles(*shape):
        return pltpu.VMEM(shape + (8, 128), F32)

    return pl.pallas_call(
        sum_kernel,
        out_shape=jax.ShapeDtypeStruct((128, 8, 128), F32),
        in_specs=[VMEM],
        out_specs=VMEM,
        scratch_shapes=[
            tiles(64), tiles(64), tiles(3, 16), tiles(16), tiles(3, 4), tiles(4, 4),
            pltpu.SemaphoreType.DMA((17,)), pltpu.SemaphoreType.DMA((17,)),
        ],
        compiler_params=pltpu.CompilerParams(vmem_limit_bytes=ROOM, collective_id=0, has_side_effects=True),
        name="gram_sum",
    )(gram)


def dense_kernel(gram_ref, s_ref, r_ref, p_ref, block_ref, search_ref, rot_ref):
    rotation(unpack(gram_ref), math.sqrt(UNKNOWNS), rot_ref)
    rot = rot_ref[...]
    for i in range(6):
        lanes = slice(256 * i, 256 * i + 256)
        tail = mm(rot[:, K:], jnp.concatenate([r_ref[:, lanes], p_ref[:, lanes]], 0))
        head = tail + mm(rot[:, :K], s_ref[:, lanes])
        for h in range(2):
            block_ref[pl.ds(2 * i + h, K, stride=12), :] = head[:, 128 * h : 128 * h + 128]
            search_ref[pl.ds(2 * i + h, K, stride=12), :] = tail[:, 128 * h : 128 * h + 128]


def shifted(block, axes, by):
    counts = [lax.axis_size(axis) for axis in ("axial", "hoop")]
    pairs = []
    for axial in range(counts[0]):
        for hoop in range(counts[1]):
            to_axial = axial + (by if "axial" in axes else 0)
            to_hoop = (hoop + (by if "hoop" in axes else 0)) % counts[1]
            if 0 <= to_axial < counts[0]:
                pairs.append((axial * counts[1] + hoop, to_axial * counts[1] + to_hoop))
    return lax.ppermute(block, ("axial", "hoop"), pairs)


def on_device(start_block, search_block, ritz_values, element_matrix, moduli, material_ids, held):
    shape = start_block.shape
    field, edge = ((K, 1536), F32), ((K, 128), F32)
    columns = [pltpu.VMEM((K * 64, 128), F32)] * 2
    start, search = start_block.reshape(1152, 128), search_block.reshape(1152, 128)
    held, ids = held.reshape(4, 128), material_ids.reshape(3, 128)
    s, p, s_edge, p_edge, weights = call(load_kernel, [field, field, edge, edge, ((96, 384), BF16)], 4, name="load")(
        start, search, held, element_matrix
    )

    def around(x, x_edge):
        return shifted(x, ("axial",), -1), shifted(x_edge, ("hoop",), -1), shifted(x_edge, ("axial", "hoop"), -1)

    s_around = around(s, s_edge)
    p_around = around(p, p_edge)
    near, after, over, after_over = call(
        image_kernel, [field, field, edge, edge], 7, columns, [VMEM] * 6 + [SMEM], name="image"
    )(s, *s_around, ids, weights, moduli)
    below = shifted(after, ("axial",), 1)
    left = shifted(over, ("hoop",), 1)
    below_left = shifted(after_over, ("axial", "hoop"), 1)
    image, r, r_edge = call(residual_kernel, [field, field, edge], 7, name="residual")(
        s, near, below, left, below_left, held, ritz_values.reshape(K, 1)
    )
    r_around = around(r, r_edge)
    gram = call(
        gram_kernel,
        [((128, 8, 128), F32)],
        13,
        columns + [pltpu.VMEM((K, 3328), F32)],
        [VMEM] * 12 + [SMEM],
        name="gram",
    )(s, image, r, *r_around, p, *p_around, ids, weights, moduli)[0]
    gram = sum_over_devices(gram)
    out = ((1152, 128), F32)
    block, search = call(dense_kernel, [out, out], 4, [pltpu.VMEM((K, 288), F32)], name="dense")(gram, s, r, p)
    return block.reshape(shape), search.reshape(shape)


def solution(mesh):
    split_field = P(None, None, None, "axial", "hoop")
    split_nodes = P(None, "axial", "hoop")
    in_specs = (split_field, split_field, P(), P(), P(), split_nodes, split_nodes)
    return jax.shard_map(
        on_device, mesh=mesh, in_specs=in_specs, out_specs=(split_field, split_field), check_vma=False
    )
```

time: 678 us -> 166 us (0.24); the launches traced: 665 us -> 165 us
  waiting for transfers between devices: 236 us -> 42 us
  local copies, waits for them, and re-layouts: 176 us -> 4.28 us
  other arithmetic: 155 us -> 0 us
  Pallas kernels: 0 us -> 99.8 us
  matrix products: 37.1 us -> 0 us
  starting transfers between devices: 44 us -> 18.2 us
  between operations: 17.1 us -> 0.78 us
    psum x1 -> x0, waiting for transfers between devices: 151 us -> none  [on_device(): cross, inner = lax.psum((cross, inner), ('axial', 'hoop'))]
    pallas_call x0 -> x6, Pallas kernels: none -> 99.8 us  [the longest x1 31.1 us: sum_over_devices(): pl.pallas_call(sum_kernel, out_shape=jax.ShapeDtypeStruct((128, 8, 128),...]
    another operation x22 -> x0, other arithmetic: 97.3 us -> none  [the longest x10 47.6 us: on_device(): system = jnp.linalg.cholesky(gram_a + shift_value * inner)]
    scatter-add x18 -> x0, local copies, waits for them, and re-layouts: 70.5 us -> none  [the longest x15 60.1 us: assemble(): total.at[:, :, dr:dr + layers, da:da + along, dh:dh + beside_all]]
    slice x36 -> x0, local copies, waits for them, and re-layouts: 44.3 us -> none  [the longest x11 19.2 us: corner_products(): ext[:, :, dr:dr + layers, da:da + along, dh:dh + beside_all]]
    ppermute x12, waiting for transfers between devices: 84.3 us -> 42 us  [shifted(): return lax.ppermute(block, ('axial', 'hoop'), pairs)]
    dot_general x8 -> x0, matrix products: 33.3 us -> none  [the longest x3 21.9 us: corner_products(): jnp.einsum('pqcd,ckdrah->pkqrah', kmat4, corners, precision=lax.Precision...]
    add x20 -> x0, other arithmetic: 28.4 us -> none  [the longest x12 18.4 us: assemble(): total.at[:, :, dr:dr + layers, da:da + along, dh:dh + beside_all]]
  transfers between devices with their start and end apart: 13 -> 12, of which waited for: 11 -> 6; matrix products, arithmetic and copies ran while one was open for 4% -> 0% of each run, Pallas kernels for 0% -> 1%
where the time goes in v1:
time: 166 us; the launch traced here: 165 us
  Pallas kernels  99.8 us (60%)
  waiting for transfers between devices  42 us (25%)
  starting transfers between devices  18.2 us (11%)
  local copies, waits for them, and re-layouts  4.28 us (3%)
    ppermute x12, waiting for transfers between devices, shifted(): return lax.ppermute(block, ('axial', 'hoop'), pairs)  42 us
    pallas_call x1, Pallas kernels, sum_over_devices(): pl.pallas_call(sum_kernel, out_shape=jax.ShapeDtypeStruct((128, 8, 128),...  31.1 us
    pallas_call x1, Pallas kernels, on_device(): call(dense_kernel, [out, out], 4, [pltpu.VMEM((K, 288), F32)], name='dense')  28.3 us
    pallas_call x1, Pallas kernels, on_device(): call(gram_kernel, [((128, 8, 128), F32)], 13, columns + [pltpu.VMEM((K, 3...  27.1 us
    ppermute x12, starting transfers between devices, shifted(): return lax.ppermute(block, ('axial', 'hoop'), pairs)  18.2 us
    pallas_call x1, Pallas kernels, on_device(): call(image_kernel, [field, field, edge, edge], 7, columns, [VMEM] * 6 + [...  11.8 us
    unnamed x15, local copies, waits for them, and re-layouts  4.18 us
  transfers between devices with their start and end apart: 12, of which 6 were waited for; matrix products, arithmetic and copies ran while one was open for 0% of the time, Pallas kernels for 1%

profile of v1, /device:TPU:1, one launch (start us, length us, event | category | flops | bytes accessed | tf_op | source)
XLA Modules:
  0.0 165.2 jit_solution(13989931494013112684)
XLA Ops:
  0.6 0.7 copy-done.3
  1.3 1.1 copy-done
  2.4 1.1 copy-done.1
  3.4 0.7 copy-done.2
  4.2 0.6 load.1
  4.7 0.0 copy-start.5
  4.7 1.3 collective-permute-start
  6.0 1.4 collective-permute-start.1
  7.5 1.3 collective-permute-start.2
  8.8 1.7 %collective-permute-done.1.edge_ref = f32[96,128]{1,0:T(8,128)S(1)} collective-permute-done((f32[96,128]{1,0:T(8,128)S(1)}, f32[96,128]{1,0:T(8,128)S(1)}, u32[]{:S(2)}, u32[]{:S(2)}) %collective-permute-start.1) | collective-permute-done | bytes 49184 | tf_op jit(solution)/shard_map/ppermute | solution.py:476
  10.5 14.1 %collective-permute-done.2.far_edge_ref = f32[96,128]{1,0:T(8,128)S(1)} collective-permute-done((f32[96,128]{1,0:T(8,128)S(1)}, f32[96,128]{1,0:T(8,128)S(1)}, u32[]{:S(2)}, u32[]{:S(2)}) %collective-permute-start.2) | collective-permute-done | bytes 49184 | tf_op jit(solution)/shard_map/ppermute | solution.py:476
  24.6 0.7 copy-done.4
  25.2 11.8 %image.1 = (f32[96,1536]{1,0:T(8,128)S(1)}, f32[96,1536]{1,0:T(8,128)}, f32[96,128]{1,0:T(8,128)S(1)}, f32[96,128]{1,0:T(8,128)S(1)}) custom-call(f32[96,1536]{1,0:T(8,128)S(1)} %get-tuple-element.16.s_ref, f32[96,1536]{1,0:T(8,128)S(1)} %collective-permute-done.far_ref, f32[96,128]{1,0:T(8,128)S(1)} %collective-permute-done.1.edge_ref, ...), custom_call_target="tpu_custom_call" | custom-call | tf_op jit(solution)/shard_map/image/pallas_call | solution.py:494
  37.0 3.1 %collective-permute-start.3 = (f32[96,1536]{1,0:T(8,128)}, f32[96,1536]{1,0:T(8,128)S(1)}, u32[]{:S(2)}, u32[]{:S(2)}) collective-permute-start(f32[96,1536]{1,0:T(8,128)} %get-tuple-element.20), channel_id=1, source_target_pairs={{0,8},{1,9},{2,10},{3,11},{4,12},{5,13},{6,14},{7,15},{8,16},{9,17... | collective-permute-start | bytes 1769480 | tf_op jit(solution)/shard_map/ppermute | solution.py:476
  40.1 0.6 collective-permute-start.4
  40.8 3.9 %collective-permute-start.5 = (f32[96,128]{1,0:T(8,128)S(1)}, f32[96,128]{1,0:T(8,128)S(1)}, u32[]{:S(2)}, u32[]{:S(2)}) collective-permute-start(f32[96,128]{1,0:T(8,128)S(1)} %get-tuple-element.22), channel_id=1, source_target_pairs={{0,9},{1,10},{2,11},{3,12},{4,13},{5,14},{6,15},{7,8},{8,17},{9,18... | collective-permute-start | bytes 147464 | tf_op jit(solution)/shard_map/ppermute | solution.py:476
  44.6 0.0 copy-start.6
  44.7 1.3 collective-permute-start.9
  46.0 0.1 copy.9.ritz_ref
  46.1 8.0 %collective-permute-done.5.below_over_ref = f32[96,128]{1,0:T(8,128)S(1)} collective-permute-done((f32[96,128]{1,0:T(8,128)S(1)}, f32[96,128]{1,0:T(8,128)S(1)}, u32[]{:S(2)}, u32[]{:S(2)}) %collective-permute-start.5) | collective-permute-done | bytes 49184 | tf_op jit(solution)/shard_map/ppermute | solution.py:476
  54.1 1.0 residual.1
  55.1 1.3 collective-permute-start.6
  56.4 0.1 collective-permute-start.10
  56.5 1.3 collective-permute-start.11
  57.8 1.1 collective-permute-start.7
  59.0 1.3 collective-permute-done.10.p_edge_ref
  60.3 1.5 collective-permute-start.8
  61.7 15.9 %collective-permute-done.11.p_far_edge_ref = f32[96,128]{1,0:T(8,128)S(1)} collective-permute-done((f32[96,128]{1,0:T(8,128)S(1)}, f32[96,128]{1,0:T(8,128)S(1)}, u32[]{:S(2)}, u32[]{:S(2)}) %collective-permute-start.11) | collective-permute-done | bytes 49184 | tf_op jit(solution)/shard_map/ppermute | solution.py:476
  77.7 1.0 collective-permute-done.8.r_far_edge_ref
  78.6 27.1 %gram.1.g_ref = f32[128,8,128]{2,1,0:T(8,128)S(1)} custom-call(f32[96,1536]{1,0:T(8,128)S(1)} %get-tuple-element.16.s_ref, f32[96,1536]{1,0:T(8,128)S(1)} %get-tuple-element.23.image_ref, f32[96,1536]{1,0:T(8,128)S(1)} %get-tuple-element.24.r_ref, f32[96,1536]{1,0:T(8,128)S(1)} %collective-permute-done.6.r_far_ref, ...), custom_call_target="tpu_custom_call" | custom-call | tf_op jit(solution)/shard_map/gram/pallas_call | solution.py:504
  105.8 31.1 %gram_sum.1.gram_ref = f32[128,8,128]{2,1,0:T(8,128)S(1)} custom-call(f32[128,8,128]{2,1,0:T(8,128)S(1)} %gram.1.g_ref), custom_call_target="tpu_custom_call" | custom-call | tf_op jit(solution)/shard_map/gram_sum/pallas_call | solution.py:441
  136.8 28.3 %dense.1 = (f32[1152,128]{1,0:T(8,128)}, f32[1152,128]{1,0:T(8,128)}) custom-call(f32[128,8,128]{2,1,0:T(8,128)S(1)} %gram_sum.1.gram_ref, f32[96,1536]{1,0:T(8,128)S(1)} %get-tuple-element.16.s_ref, f32[96,1536]{1,0:T(8,128)S(1)} %get-tuple-element.24.r_ref, f32[96,1536]{1,0:T(8,128)S(1)} %get-tuple-element.26.p_ref), custom_call_target="tpu_custom_call" | custom-call | tf_op jit(solution)/shard_map/dense/pallas_call | solution.py:514
  (14 shorter events, 0.0 us)
Async XLA Ops:
  0.6 0.7 copy-start.3
  1.3 1.1 copy-start
  2.4 1.1 copy-start.1
  3.4 0.7 copy-start.2
  4.7 4.0 %copy-start.5 = (s32[3,1,128]{2,1,0:T(1,128)S(1)}, s32[3,1,128]{2,1,0:T(1,128)}, u32[]{:S(2)}) copy-start(s32[3,1,128]{2,1,0:T(1,128)} %param.12) | copy-start | bytes 4612
  4.7 19.8 %collective-permute-start = (f32[96,1536]{1,0:T(8,128)S(1)}, f32[96,1536]{1,0:T(8,128)S(1)}, u32[]{:S(2)}, u32[]{:S(2)}) collective-permute-start(f32[96,1536]{1,0:T(8,128)S(1)} %get-tuple-element.16.s_ref), channel_id=1, source_target_pairs={{8,0},{9,1},{10,2},{11,3},{12,4},{13,5},{14,6},{15,7},{16,8},{17,9... | collective-permute-start | bytes 1769480 | tf_op jit(solution)/shard_map/ppermute | solution.py:476
  6.0 4.5 %collective-permute-start.1 = (f32[96,128]{1,0:T(8,128)S(1)}, f32[96,128]{1,0:T(8,128)S(1)}, u32[]{:S(2)}, u32[]{:S(2)}) collective-permute-start(f32[96,128]{1,0:T(8,128)S(1)} %get-tuple-element.17), channel_id=1, source_target_pairs={{0,7},{1,0},{2,1},{3,2},{4,3},{5,4},{6,5},{7,6},{8,15},{9,8},{10,9... | collective-permute-start | bytes 147464 | tf_op jit(solution)/shard_map/ppermute | solution.py:476
  7.5 17.1 %collective-permute-start.2 = (f32[96,128]{1,0:T(8,128)S(1)}, f32[96,128]{1,0:T(8,128)S(1)}, u32[]{:S(2)}, u32[]{:S(2)}) collective-permute-start(f32[96,128]{1,0:T(8,128)S(1)} %get-tuple-element.17), channel_id=1, source_target_pairs={{8,7},{9,0},{10,1},{11,2},{12,3},{13,4},{14,5},{15,6},{16,15},{17,... | collective-permute-start | bytes 147464 | tf_op jit(solution)/shard_map/ppermute | solution.py:476
  24.6 0.7 copy-start.4
  37.0 17.1 %collective-permute-start.3 = (f32[96,1536]{1,0:T(8,128)}, f32[96,1536]{1,0:T(8,128)S(1)}, u32[]{:S(2)}, u32[]{:S(2)}) collective-permute-start(f32[96,1536]{1,0:T(8,128)} %get-tuple-element.20), channel_id=1, source_target_pairs={{0,8},{1,9},{2,10},{3,11},{4,12},{5,13},{6,14},{7,15},{8,16},{9,17... | collective-permute-start | bytes 1769480 | tf_op jit(solution)/shard_map/ppermute | solution.py:476
  40.1 5.9 %collective-permute-start.4 = (f32[96,128]{1,0:T(8,128)S(1)}, f32[96,128]{1,0:T(8,128)S(1)}, u32[]{:S(2)}, u32[]{:S(2)}) collective-permute-start(f32[96,128]{1,0:T(8,128)S(1)} %get-tuple-element.21), channel_id=1, source_target_pairs={{0,1},{1,2},{2,3},{3,4},{4,5},{5,6},{6,7},{7,0},{8,9},{9,10},{10,1... | collective-permute-start | bytes 147464 | tf_op jit(solution)/shard_map/ppermute | solution.py:476
  40.8 13.3 %collective-permute-start.5 = (f32[96,128]{1,0:T(8,128)S(1)}, f32[96,128]{1,0:T(8,128)S(1)}, u32[]{:S(2)}, u32[]{:S(2)}) collective-permute-start(f32[96,128]{1,0:T(8,128)S(1)} %get-tuple-element.22), channel_id=1, source_target_pairs={{0,9},{1,10},{2,11},{3,12},{4,13},{5,14},{6,15},{7,8},{8,17},{9,18... | collective-permute-start | bytes 147464 | tf_op jit(solution)/shard_map/ppermute | solution.py:476
  44.6 1.3 copy-start.6
  44.7 33.0 %collective-permute-start.9 = (f32[96,1536]{1,0:T(8,128)S(1)}, f32[96,1536]{1,0:T(8,128)S(1)}, u32[]{:S(2)}, u32[]{:S(2)}) collective-permute-start(f32[96,1536]{1,0:T(8,128)S(1)} %get-tuple-element.26.p_ref), channel_id=1, source_target_pairs={{8,0},{9,1},{10,2},{11,3},{12,4},{13,5},{14,6},{15,7},{16,8},{17,9... | collective-permute-start | bytes 1769480 | tf_op jit(solution)/shard_map/ppermute | solution.py:476
  55.1 23.5 %collective-permute-start.6 = (f32[96,1536]{1,0:T(8,128)S(1)}, f32[96,1536]{1,0:T(8,128)S(1)}, u32[]{:S(2)}, u32[]{:S(2)}) collective-permute-start(f32[96,1536]{1,0:T(8,128)S(1)} %get-tuple-element.24.r_ref), channel_id=1, source_target_pairs={{8,0},{9,1},{10,2},{11,3},{12,4},{13,5},{14,6},{15,7},{16,8},{17,9... | collective-permute-start | bytes 1769480 | tf_op jit(solution)/shard_map/ppermute | solution.py:476
  56.4 3.8 %collective-permute-start.10 = (f32[96,128]{1,0:T(8,128)S(1)}, f32[96,128]{1,0:T(8,128)S(1)}, u32[]{:S(2)}, u32[]{:S(2)}) collective-permute-start(f32[96,128]{1,0:T(8,128)S(1)} %get-tuple-element.27), channel_id=1, source_target_pairs={{0,7},{1,0},{2,1},{3,2},{4,3},{5,4},{6,5},{7,6},{8,15},{9,8},{10,9... | collective-permute-start | bytes 147464 | tf_op jit(solution)/shard_map/ppermute | solution.py:476
  56.5 21.1 %collective-permute-start.11 = (f32[96,128]{1,0:T(8,128)S(1)}, f32[96,128]{1,0:T(8,128)S(1)}, u32[]{:S(2)}, u32[]{:S(2)}) collective-permute-start(f32[96,128]{1,0:T(8,128)S(1)} %get-tuple-element.27), channel_id=1, source_target_pairs={{8,7},{9,0},{10,1},{11,2},{12,3},{13,4},{14,5},{15,6},{16,15},{17,... | collective-permute-start | bytes 147464 | tf_op jit(solution)/shard_map/ppermute | solution.py:476
  57.8 19.8 %collective-permute-start.7 = (f32[96,128]{1,0:T(8,128)S(1)}, f32[96,128]{1,0:T(8,128)S(1)}, u32[]{:S(2)}, u32[]{:S(2)}) collective-permute-start(f32[96,128]{1,0:T(8,128)S(1)} %get-tuple-element.25), channel_id=1, source_target_pairs={{0,7},{1,0},{2,1},{3,2},{4,3},{5,4},{6,5},{7,6},{8,15},{9,8},{10,9... | collective-permute-start | bytes 147464 | tf_op jit(solution)/shard_map/ppermute | solution.py:476
  60.3 18.4 %collective-permute-start.8 = (f32[96,128]{1,0:T(8,128)S(1)}, f32[96,128]{1,0:T(8,128)S(1)}, u32[]{:S(2)}, u32[]{:S(2)}) collective-permute-start(f32[96,128]{1,0:T(8,128)S(1)} %get-tuple-element.25), channel_id=1, source_target_pairs={{8,7},{9,0},{10,1},{11,2},{12,3},{13,4},{14,5},{15,6},{16,15},{17,... | collective-permute-start | bytes 147464 | tf_op jit(solution)/shard_map/ppermute | solution.py:476

commit v2 on v1

v2 whole, which is shorter than its diff:
```python
import functools
import math

import jax
import jax.numpy as jnp
from jax import lax
from jax.experimental import pallas as pl
from jax.experimental.pallas import tpu as pltpu
from jax.sharding import PartitionSpec as P

HI = lax.Precision.HIGHEST
MESH = pl.DeviceIdType.MESH
K = 96
F32 = jnp.float32
BF16 = jnp.bfloat16
VMEM = pl.BlockSpec(memory_space=pltpu.VMEM)
SMEM = pl.BlockSpec(memory_space=pltpu.SMEM)
ROOM = 48 * 2**20
UNKNOWNS = 196608
UNROLL = 2
COPIES = 38


def mm(a, b):
    return lax.dot_general(a, b, (((1,), (0,)), ((), ())), precision=HI, preferred_element_type=jnp.float32)

def mm_t(a, b):
    return lax.dot_general(a, b, (((0,), (0,)), ((), ())), precision=HI, preferred_element_type=jnp.float32)


def sweep(block, factor):
    lane = lax.broadcasted_iota(jnp.int32, (8, 128), 1)
    sub = lax.broadcasted_iota(jnp.int32, (8, 128), 0)
    tiles = [block[8 * t : 8 * t + 8, :] for t in range(12)]
    found = []
    for group in range(24):
        p = 4 * group
        home, low = p // 8, p % 8
        cols = [[jnp.broadcast_to(tile[:, p + j : p + j + 1], (8, 128)) for tile in tiles] for j in range(4)]
        rows = [jnp.broadcast_to(tiles[home][low + j : low + j + 1, :], (8, 128)) for j in range(4)]

        def entry(i, j):
            return jnp.broadcast_to(cols[j][home][low + i : low + i + 1, :], (8, 128))

        a00, a01, a11 = entry(0, 0), entry(0, 1), entry(1, 1)
        b00, b01, b10, b11 = entry(0, 2), entry(0, 3), entry(1, 2), entry(1, 3)
        c00, c01, c11 = entry(2, 2), entry(2, 3), entry(3, 3)
        ia = 1.0 / (a00 * a11 - a01 * a01)
        h00, h01, h11 = a11 * ia, -a01 * ia, a00 * ia
        x00, x01 = h00 * b00 + h01 * b10, h00 * b01 + h01 * b11
        x10, x11 = h01 * b00 + h11 * b10, h01 * b01 + h11 * b11
        s00 = c00 - (b00 * x00 + b10 * x10)
        s01 = c01 - (b00 * x01 + b10 * x11)
        s11 = c11 - (b01 * x01 + b11 * x11)
        ic = 1.0 / (s00 * s11 - s01 * s01)
        g00, g01, g11 = s11 * ic, -s01 * ic, s00 * ic
        picked = (lane >= p) & (lane < p + 4)
        full = [jnp.where(picked, jnp.where(lane == p + j, 1.0, 0.0), rows[j]) for j in range(4)]
        u0 = full[2] - (x00 * full[0] + x10 * full[1])
        u1 = full[3] - (x01 * full[0] + x11 * full[1])
        n2 = g00 * u0 + g01 * u1
        n3 = g01 * u0 + g11 * u1
        v0 = h00 * full[0] + h01 * full[1]
        v1 = h01 * full[0] + h11 * full[1]
        n0 = v0 - (x00 * n2 + x01 * n3)
        n1 = v1 - (x10 * n2 + x11 * n3)
        new = [n0, n1, n2, n3]
        if factor:
            left = [jnp.where(lane < p + 4, f, 0.0) for f in full]
            w0 = lax.rsqrt(a00)
            l0 = left[0] * w0
            e1 = a11 - a01 * a01 / a00
            l1 = (left[1] - (a01 / a00) * left[0]) * lax.rsqrt(e1)
            y0 = jnp.where(lane < p + 4, u0, 0.0)
            y1 = jnp.where(lane < p + 4, u1, 0.0)
            l2 = y0 * lax.rsqrt(s00)
            l3 = (y1 - (s01 / s00) * y0) * lax.rsqrt(s11 - s01 * s01 / s00)
            found.append([l0, l1, l2, l3])
        fresh = []
        for t, tile in enumerate(tiles):
            kept = jnp.where(picked, 0.0, tile)
            if t == home:
                here = (sub >= low) & (sub < low + 4)
                kept = jnp.where(here, 0.0, kept)
                q = [jnp.where(here, jnp.where(sub == low + j, -1.0, 0.0), cols[j][t]) for j in range(4)]
            else:
                q = [cols[j][t] for j in range(4)]
            fresh.append(kept - ((q[0] * n0 + q[1] * n1) + (q[2] * n2 + q[3] * n3)))
        tiles = fresh
    if factor:
        out = []
        for t in range(12):
            eight = found[2 * t] + found[2 * t + 1]
            tile = eight[0]
            for s in range(1, 8):
                tile = jnp.where(sub == s, eight[s], tile)
            out.append(tile)
        return jnp.concatenate(out, 0)
    return jnp.concatenate(tiles, 0)


def diagonal(block):
    lane = lax.broadcasted_iota(jnp.int32, (K, 128), 1)
    row = lax.broadcasted_iota(jnp.int32, (K, 128), 0)
    only = jnp.where(lane == row, block, 0.0)
    down = jnp.sum(only, 1, keepdims=True)
    along = jnp.sum(only, 0, keepdims=True)
    return lax.rsqrt(down), lax.rsqrt(jnp.where(along == 0.0, 1.0, along))


def cut(block):
    return block[:, :K]


def pad(block):
    return jnp.concatenate([block, jnp.zeros((block.shape[0], 128 - block.shape[1]), jnp.float32)], 1)


def rotation(gram, scale, rot_ref):
    b = [gram[i] for i in range(6)]
    a = [gram[6 + i] for i in range(6)]
    m = [x + y for x, y in zip(a, b)]
    d0, e0 = diagonal(m[0])
    d1, e1 = diagonal(m[3])
    d2, e2 = diagonal(m[5])
    m11, m12, m13 = m[0] * d0 * e0, m[1] * d0 * e1, m[2] * d0 * e2
    m22, m23, m33 = m[3] * d1 * e1, m[4] * d1 * e2, m[5] * d2 * e2
    bsr_t, bsp_t, brp_t = (pad(cut(x).T) for x in (b[1], b[2], b[4]))
    f1, f2, f3 = b[0] * d0, bsr_t * d1, bsp_t * d2
    i1 = sweep(m11, False)
    t1 = mm(cut(i1), jnp.concatenate([m12, m13, f1], 1))
    t12, t13, y1 = t1[:, :128], t1[:, 128:256], t1[:, 256:]
    s2 = jnp.concatenate([m22, m23, f2], 1) - mm(cut(m12).T, t1)
    s3 = jnp.concatenate([m33, f3], 1) - mm(cut(m13).T, t1[:, 128:])
    i2 = sweep(s2[:, :128], False)
    m23 = s2[:, 128:256]
    t2 = mm(cut(i2), s2[:, 128:])
    s3 = s3 - mm(cut(m23).T, t2)
    i3 = sweep(s3[:, :128], False)
    w3 = mm(cut(i3), s3[:, 128:])
    w2 = t2[:, 128:] - mm(cut(t2), w3)
    w1 = y1 - mm(jnp.concatenate([cut(t12), cut(t13)], 1), jnp.concatenate([w2, w3], 0))
    w = jnp.concatenate([w1 * d0, w2 * d1, w3 * d2], 0)
    big = jnp.concatenate(
        [
            jnp.concatenate([cut(b[0]), cut(b[1]), cut(b[2])], 1),
            jnp.concatenate([cut(bsr_t), cut(b[3]), cut(b[4])], 1),
            jnp.concatenate([cut(bsp_t), cut(brp_t), cut(b[5])], 1),
        ],
        0,
    )
    wt = cut(w).T
    small = mm(wt, mm(big, w))
    ds, es = diagonal(small)
    inv = sweep(small * ds * es, True) * es
    rot_ref[...] = mm(cut(inv), wt) * scale


def mm_nt(a, b):
    return lax.dot_general(a, b, (((1,), (1,)), ((), ())), precision=HI, preferred_element_type=F32)


def split(x):
    high = x.astype(BF16)
    rest = x - high.astype(F32)
    middle = rest.astype(BF16)
    low = (rest - middle.astype(F32)).astype(BF16)
    return high, middle, low


def stencil(kmat):
    def rows_of(shape, axis):
        at = lax.broadcasted_iota(jnp.int32, shape, axis)
        low, high = at % 8, at // 8
        dh, high = high % 2, high // 2
        return low // 3, low % 3, dh, high % 3, high // 3, low < 6

    def columns_of(shape, axis):
        at = lax.broadcasted_iota(jnp.int32, shape, axis)
        low, high = at % 8, at // 8
        return low // 3, low % 3, high // 4, high % 4, low < 6

    da, q, dh, _, dr, real = rows_of((96, 24), 0)
    corner = lax.broadcasted_iota(jnp.int32, (96, 24), 1)
    pick = jnp.where(real & (corner == 3 * (4 * dr + 2 * da + dh) + q), 1.0, 0.0)
    picked = mm(pick, kmat)
    layer = rows_of((96, 64), 0)[3]
    node = columns_of((96, 64), 1)[3]
    total = jnp.zeros((96, 64), F32)
    for dr in range(2):
        da, q, dh, _, real = columns_of((24, 64), 1)
        corner = lax.broadcasted_iota(jnp.int32, (24, 64), 0)
        place = jnp.where(real & (corner == 3 * (4 * dr + 2 * da + dh) + q), 1.0, 0.0)
        total = total + jnp.where(node == layer + dr, mm(picked, place), 0.0)
    high, middle, low = split(total)
    return jnp.concatenate([high, high, high, middle, middle, low], 1)


def lanes_of(rows):
    return lax.broadcasted_iota(jnp.int32, (rows, 128), 1)


def turn(x, by):
    return pltpu.roll(x, by % 128, 1) if by % 128 else x


def swap(tiles):
    lane = lanes_of(tiles[0].shape[0])
    front, even = lane < 64, (lane // 32) % 2 == 0
    a, b, c, d = tiles
    a, c = jnp.where(front, a, turn(c, 64)), jnp.where(front, turn(a, 64), c)
    b, d = jnp.where(front, b, turn(d, 64)), jnp.where(front, turn(b, 64), d)
    a, b = jnp.where(even, a, turn(b, 32)), jnp.where(even, turn(a, 96), b)
    c, d = jnp.where(even, c, turn(d, 32)), jnp.where(even, turn(c, 96), d)
    return a, b, c, d


def tile(ref, i):
    return ref[:, 128 * i : 128 * i + 128]


def set_tile(ref, i, value):
    ref[:, 128 * i : 128 * i + 128] = value


def pack(field_ref, pack_ref):
    for q in range(3):
        for to, value in enumerate(swap([tile(field_ref, 4 * q + r) for r in range(4)])):
            pack_ref[to, 96 * q : 96 * q + 96, :] = value


def unpack(came_ref, field_ref):
    for q in range(3):
        for r, value in enumerate(swap([came_ref[j, 96 * q : 96 * q + 96, :] for j in range(4)])):
            set_tile(field_ref, 4 * q + r, value)


def first_nodes(field_ref, layer_ref, edge_ref):
    lane = lanes_of(K)
    edge = jnp.zeros((K, 128), F32)
    for q in range(3):
        layer = jnp.zeros((K, 128), F32)
        for r in range(4):
            value = tile(field_ref, 4 * q + r)
            layer = jnp.where(lane // 32 == r, turn(value, 32 * r), layer)
            edge = jnp.where(lane % 32 == 4 * q + r, turn(value, 4 * q + r), edge)
        layer_ref[96 * q : 96 * q + 96, :] = layer
    edge_ref[...] = edge


def put(columns_ref, field_ref, layer_ref, edge, far_edge, top):
    lane = lanes_of(K)
    for q in range(3):
        for r in range(4):
            i = 4 * q + r
            near = tile(field_ref, i)
            ahead = jnp.where(top, 0.0, turn(layer_ref[96 * q : 96 * q + 96, :], 32 * (3 - r)))
            far = jnp.where(lane < 96, turn(near, 96), ahead)
            for da, (value, side) in enumerate(((near, edge), (far, far_edge))):
                at = 8 * r + 3 * da + q
                columns_ref[pl.ds(at, K, stride=64), :] = value
                moved = jnp.where(lane % 32 == 31, turn(side, 31 - i), turn(value, 127))
                columns_ref[pl.ds(32 + at, K, stride=64), :] = moved


def far_edges(edge, corner, top):
    lane = lanes_of(K)
    corner = jnp.where(top, 0.0, jnp.where(lane < 96, 0.0, turn(corner, 96)))
    return corner, jnp.where(lane < 96, turn(edge, 96), corner)


def products(columns_ref, image_ref, stencil_ref, coef):
    weights = stencil_ref[...]
    coef = [jnp.broadcast_to(coef[r : r + 1], (8, 128)) for r in range(3)]
    wide = 8

    def step(group, carry):
        base = pl.multiple_of(64 * wide * group, 64 * wide)
        some = columns_ref[pl.ds(base, 64 * wide), :]
        high, middle, low = split(jnp.concatenate([some[64 * c : 64 * c + 64] for c in range(wide)], 1))
        stack = jnp.concatenate([high, middle, low, high, middle, high], 0)
        terms = jnp.dot(weights, stack, preferred_element_type=F32)
        for c in range(wide):
            term = terms[:, 128 * c : 128 * c + 128]

            def part(dr, r, dh):
                at = 8 * ((dr * 3 + r) * 2 + dh)
                return term[at : at + 8] * coef[r]

            values = []
            for dh in range(2):
                for node in range(4):
                    parts = [part(dr, node - dr, dh) for dr in range(2) if 0 <= node - dr < 3]
                    values.append(parts[0] if len(parts) == 1 else parts[0] + parts[1])
            image_ref[pl.ds(base + 64 * c, 64), :] = jnp.concatenate(values, 0)
        return carry

    lax.fori_loop(0, K // wide, step, 0, unroll=UNROLL)


def take(image_ref, wide_ref):
    lane = lanes_of(K)
    over, far_over = jnp.zeros((K, 128), F32), jnp.zeros((K, 128), F32)
    for q in range(3):
        layer = jnp.zeros((K, 128), F32)
        for r in range(4):
            i = 4 * q + r
            at = 8 * r + q

            def shifted_sum(at):
                second = image_ref[pl.ds(32 + at, K, stride=64), :]
                first = image_ref[pl.ds(at, K, stride=64), :]
                return first + jnp.where(lane % 32 == 0, 0.0, turn(second, 1)), turn(second, i - 31)

            near, out = shifted_sum(at)
            far, far_out = shifted_sum(at + 3)
            over = jnp.where(lane % 32 == i, out, over)
            far_over = jnp.where(lane % 32 == i, far_out, far_over)
            set_tile(wide_ref, i, near + jnp.where(lane < 32, 0.0, turn(far, 32)))
            layer = jnp.where(lane // 32 == r, turn(far, 32 * (r - 3)), layer)
        set_tile(wide_ref, 12 + q, layer)
    set_tile(wide_ref, 15, over + jnp.where(lane < 32, 0.0, turn(far_over, 32)))
    set_tile(wide_ref, 16, jnp.where(lane < 96, 0.0, far_over))


def front_kernel(
    start_hbm, search_hbm, held_ref, ids_ref, kmat_ref, ritz_ref, moduli_ref,
    gram_ref, s_out, r_out, p_out,
    start_in, search_in, stencil_ref, s, r, p, image_s, columns, image, wide, blocks,
    s_pack, p_pack, r_pack, s_came, p_came, r_came,
    s_layer, r_layer, p_layer, s_edge, r_edge, p_edge,
    s_ahead, r_ahead, p_ahead, s_side, r_side, p_side, s_corner, r_corner, p_corner,
    back, back_over, back_corner, back_came, over_came, corner_came,
    whole, g, from_core, half, from_x, quarter, from_y, from_z,
    local, send, recv,
):
    axial, hoop = lax.axis_index("axial"), lax.axis_index("hoop")
    z, x = axial // 4, axial % 4
    y, core = hoop // 2, hoop % 2
    top, bottom = z == 3, z == 0
    lane = lanes_of(K)

    def at(z, x, y, core):
        return (z * 4 + x, y * 2 + core)

    def around(dz, ds):
        sector = (hoop * 4 + x + ds + 32) % 32
        return ((z + dz + 4) % 4 * 4 + sector % 4, sector // 4)

    peers = {
        "core": [at(z, x, y, 1 - core)],
        "x": [at(z, (x + d) % 4, y, core) for d in (1, 2, 3)],
        "y": [at(z, x, (y + d) % 4, core) for d in (1, 2, 3)],
        "z": [at((z + d) % 4, x, y, core) for d in (1, 2, 3)],
        "hoop": [around(0, 1), around(0, -1), around(1, 1), around(-1, -1)],
    }
    loads = [
        pltpu.make_async_copy(start_hbm, start_in, local.at[0]),
        pltpu.make_async_copy(search_hbm, search_in, local.at[1]),
    ]
    for load in loads:
        load.start()
    barrier = pltpu.get_barrier_semaphore()
    count = 0
    for group in peers.values():
        for peer in group:
            pl.semaphore_signal(barrier, inc=1, device_id=peer, device_id_type=MESH)
            count += 1
    used = [0]

    def copy(source, target, peer):
        index = used[0]
        used[0] += 1
        made = pltpu.make_async_remote_copy(
            src_ref=source, dst_ref=target, send_sem=send.at[index], recv_sem=recv.at[index],
            device_id=peer, device_id_type=MESH,
        )
        made.start()
        return made

    def finish(copies):
        for made in copies:
            made.wait()

    def exchange(pack_ref, came_ref):
        copies = []
        for d in (1, 2, 3):
            copies.append(copy(pack_ref.at[(x + d) % 4], came_ref.at[x], peers["x"][d - 1]))
        return copies

    def forward(layer, edge, ahead, side, corner):
        return [
            copy(layer, ahead, around(-1, 0)),
            copy(edge, side, around(0, -1)),
            copy(edge, corner, around(-1, -1)),
        ]

    ids = ids_ref[...]
    coef = jnp.zeros(ids.shape, F32)
    for material in range(3):
        coef = coef + jnp.where(ids == material, moduli_ref[material], 0.0)
    free = (1 - held_ref[...]).astype(F32)
    row = lax.broadcasted_iota(jnp.int32, (8, 128), 0)
    notes = []
    for node in range(4):
        note = jnp.where(row == 0, free[node : node + 1], 0.0)
        notes.append(jnp.where(row == 1, coef[node : node + 1], note) if node < 3 else note)
    for to, value in enumerate(swap(notes)):
        s_pack[to, 288:296, :] = value

    def mask_in(source, field_out):
        for i in range(12):
            set_tile(field_out, i, source[pl.ds(i, K, stride=12), :] * free[i % 4 : i % 4 + 1])

    loads[0].wait()
    mask_in(start_in, s_out)
    pack(s_out, s_pack)
    pl.semaphore_wait(barrier, count)
    flying = exchange(s_pack, s_came)
    s_came[x] = s_pack[x]
    stencil_ref[...] = stencil(kmat_ref[...])
    zero = jnp.zeros((K, 128), F32)
    for high in range(8):
        for low in (6, 7):
            columns[pl.ds(8 * high + low, K, stride=64), :] = zero
    loads[1].wait()
    mask_in(search_in, p_out)
    pack(p_out, p_pack)
    finish(flying)

    unpack(s_came, s)
    notes = swap([s_came[j, 288:296, :] for j in range(4)])
    free = [note[0:1] for note in notes]
    coef = jnp.concatenate([note[1:2] for note in notes[:3]], 0)
    first_nodes(s, s_layer, s_edge)
    flying = forward(s_layer, s_edge, s_ahead, s_side, s_corner)
    p_flying = exchange(p_pack, p_came)
    p_came[x] = p_pack[x]

    def keep(index, value):
        blocks[index, :, 0:K] = value

    keep(0, mm_nt(s[...], s[...]))
    finish(flying)
    corner, far_edge = far_edges(s_side[...], s_corner[...], top)
    put(columns, s, s_ahead, s_side[...], far_edge, top)
    products(columns, image, stencil_ref, coef)
    take(image, wide)
    for q in range(3):
        back[96 * q : 96 * q + 96, :] = tile(wide, 12 + q)
    back_over[...] = tile(wide, 15)
    back_corner[...] = tile(wide, 16)
    flying = [
        copy(back, back_came, around(1, 0)),
        copy(back_over, over_came, around(0, 1)),
        copy(back_corner, corner_came, around(1, 1)),
    ]

    finish(p_flying)
    unpack(p_came, p)
    first_nodes(p, p_layer, p_edge)
    p_flying = forward(p_layer, p_edge, p_ahead, p_side, p_corner)
    keep(2, mm_nt(s[...], p[...]))
    keep(5, mm_nt(p[...], p[...]))
    finish(flying)

    over = over_came[...] + jnp.where(bottom, 0.0, jnp.where(lane < 32, turn(corner_came[...], 32), 0.0))
    for q in range(3):
        below = jnp.where(bottom, 0.0, back_came[96 * q : 96 * q + 96, :])
        for node in range(4):
            i = 4 * q + node
            value = tile(wide, i) + jnp.where(lane < 32, turn(below, -32 * node), 0.0)
            value = (value + jnp.where(lane % 32 == 0, turn(over, -i), 0.0)) * free[node]
            set_tile(image_s, i, value)
            set_tile(r, i, value - ritz_ref[...] * tile(s, i))
    first_nodes(r, r_layer, r_edge)
    flying = forward(r_layer, r_edge, r_ahead, r_side, r_corner)
    pack(r, r_pack)
    r_flying = exchange(r_pack, r_came)
    r_came[x] = r_pack[x]

    def ext(field, ahead, side, corner):
        layers = [jnp.where(top, 0.0, ahead[96 * q : 96 * q + 96, :]) for q in range(3)]
        return jnp.concatenate([field[...]] + layers + [side[...], corner], 1)

    finish(p_flying)
    corner, far_edge = far_edges(p_side[...], p_corner[...], top)
    put(columns, p, p_ahead, p_side[...], far_edge, top)
    products(columns, image, stencil_ref, coef)
    take(image, wide)
    p_ext = ext(p, p_ahead, p_side, corner)
    keep(11, mm_nt(wide[...], p_ext))
    for index, left, right in ((6, image_s, s), (7, image_s, r), (8, image_s, p), (1, s, r), (3, r, r), (4, r, p)):
        keep(index, mm_nt(left[...], right[...]))
    finish(flying)
    corner, far_edge = far_edges(r_side[...], r_corner[...], top)
    put(columns, r, r_ahead, r_side[...], far_edge, top)
    products(columns, image, stencil_ref, coef)
    take(image, wide)
    keep(9, mm_nt(wide[...], ext(r, r_ahead, r_side, corner)))
    keep(10, mm_nt(wide[...], ext(p, p_ahead, p_side, far_edges(p_side[...], p_corner[...], top)[0])))

    for group in range(3):
        extra = jnp.where(lane < K, blocks[9 + group], 0.0)
        for j in range(3):
            both = jnp.where(lane < K, blocks[3 * group + j], turn(extra, 96 - 32 * j))
            first = 12 * (3 * group + j)
            g[first : first + 12] = both.reshape(12, 8, 128)
    g[108:128] = jnp.zeros((20, 8, 128), F32)

    finish([copy(g.at[pl.ds((1 - core) * 64, 64)], from_core, peers["core"][0])])
    half[...] = g[pl.ds(core * 64, 64)] + from_core[...]
    finish([copy(half.at[pl.ds((x + d) % 4 * 16, 16)], from_x.at[d - 1], peers["x"][d - 1]) for d in (1, 2, 3)])
    quarter[...] = (half[pl.ds(x * 16, 16)] + from_x[0]) + (from_x[1] + from_x[2])
    finish([copy(quarter.at[pl.ds((y + d) % 4 * 4, 4)], from_y.at[d - 1], peers["y"][d - 1]) for d in (1, 2, 3)])
    from_z[z] = (quarter[pl.ds(y * 4, 4)] + from_y[0]) + (from_y[1] + from_y[2])
    finish([copy(from_z.at[z], from_z.at[z], peer) for peer in peers["z"]])
    base = core * 64 + x * 16 + y * 4
    whole[pl.ds(base, 4)] = (from_z[0] + from_z[1]) + (from_z[2] + from_z[3])
    for axis, first, size in (("y", base, 4), ("x", core * 64 + x * 16, 16), ("core", core * 64, 64)):
        part = whole.at[pl.ds(first, size)]
        finish([copy(part, part, peer) for peer in peers[axis]])
    gram_ref[...] = whole[...]
    finish(r_flying)
    unpack(r_came, r_out)


def front(start, search, held, ids, kmat, ritz, moduli):
    def rows(*shape):
        return pltpu.VMEM(shape + (128,), F32)

    field = pltpu.VMEM((K, 1536), F32)
    anywhere = pl.BlockSpec(memory_space=pl.ANY)
    return pl.pallas_call(
        front_kernel,
        out_shape=[jax.ShapeDtypeStruct((128, 8, 128), F32)] + [jax.ShapeDtypeStruct((K, 1536), F32)] * 3,
        in_specs=[anywhere] * 2 + [VMEM] * 4 + [SMEM],
        out_specs=[VMEM] * 4,
        scratch_shapes=[rows(1152)] * 2
        + [pltpu.VMEM((96, 384), BF16)]
        + [field] * 4
        + [rows(K * 64)] * 2
        + [pltpu.VMEM((K, 17 * 128), F32), rows(12, K)]
        + [rows(4, 296), rows(4, 288), rows(4, 288)] * 2
        + [rows(288)] * 3 + [rows(K)] * 3
        + [rows(288)] * 3 + [rows(K)] * 6
        + [rows(288), rows(K), rows(K)] * 2
        + [rows(n, 8) for n in (128, 128, 64, 64)]
        + [rows(3, 16, 8), rows(16, 8), rows(3, 4, 8), rows(4, 4, 8)]
        + [pltpu.SemaphoreType.DMA((2,)), pltpu.SemaphoreType.DMA((COPIES,)), pltpu.SemaphoreType.DMA((COPIES,))],
        compiler_params=pltpu.CompilerParams(vmem_limit_bytes=ROOM, collective_id=0, has_side_effects=True),
        name="front",
    )(start, search, held, ids, kmat, ritz, moduli)


def unpack_gram(gram_ref):
    lane = lanes_of(K)
    blocks = [None] * 12
    for group in range(3):
        extra = jnp.zeros((K, 128), F32)
        for j in range(3):
            first = 12 * (3 * group + j)
            both = gram_ref[first : first + 12].reshape(K, 128)
            blocks[3 * group + j] = jnp.where(lane < K, both, 0.0)
            here = (lane >= 32 * j) & (lane < 32 * j + 32)
            extra = jnp.where(here, turn(both, 32 + 32 * j), extra)
        blocks[9 + group] = extra
    return blocks


def dense_kernel(gram_ref, s_ref, r_ref, p_ref, block_ref, search_ref, rot_ref):
    rotation(unpack_gram(gram_ref), math.sqrt(UNKNOWNS), rot_ref)
    rot = rot_ref[...]
    for i in range(6):
        lanes = slice(256 * i, 256 * i + 256)
        tail = mm(rot[:, K:], jnp.concatenate([r_ref[:, lanes], p_ref[:, lanes]], 0))
        head = tail + mm(rot[:, :K], s_ref[:, lanes])
        for h in range(2):
            block_ref[pl.ds(2 * i + h, K, stride=12), :] = head[:, 128 * h : 128 * h + 128]
            search_ref[pl.ds(2 * i + h, K, stride=12), :] = tail[:, 128 * h : 128 * h + 128]


def dense(gram, s, r, p):
    return pl.pallas_call(
        dense_kernel,
        out_shape=[jax.ShapeDtypeStruct((1152, 128), F32)] * 2,
        in_specs=[VMEM] * 4,
        out_specs=[VMEM] * 2,
        scratch_shapes=[pltpu.VMEM((K, 288), F32)],
        compiler_params=pltpu.CompilerParams(vmem_limit_bytes=ROOM),
        name="dense",
    )(gram, s, r, p)


def on_device(start_block, search_block, ritz_values, element_matrix, moduli, material_ids, held):
    shape = start_block.shape
    gram, s, r, p = front(
        start_block.reshape(1152, 128), search_block.reshape(1152, 128), held.reshape(4, 128),
        material_ids.reshape(3, 128), element_matrix, ritz_values.reshape(K, 1), moduli,
    )
    block, search = dense(gram, s, r, p)
    return block.reshape(shape), search.reshape(shape)


def solution(mesh):
    split_field = P(None, None, None, "axial", "hoop")
    split_nodes = P(None, "axial", "hoop")
    in_specs = (split_field, split_field, P(), P(), P(), split_nodes, split_nodes)
    return jax.shard_map(
        on_device, mesh=mesh, in_specs=in_specs, out_specs=(split_field, split_field), check_vma=False
    )
```

time: 166 us -> 120 us (0.72)
  waiting for transfers between devices: 42 us -> 0 us
  starting transfers between devices: 18.2 us -> 0 us
  Pallas kernels: 99.8 us -> 114 us
    ppermute x12 -> x0, waiting for transfers between devices: 42 us -> none  [shifted(): return lax.ppermute(block, ('axial', 'hoop'), pairs)]
    ppermute x12 -> x0, starting transfers between devices: 18.2 us -> none  [shifted(): return lax.ppermute(block, ('axial', 'hoop'), pairs)]
    pallas_call x6 -> x2, Pallas kernels: 99.8 us -> 114 us  [the longest x1 86.2 us: front(): pl.pallas_call(front_kernel, out_shape=[jax.ShapeDtypeStruct((128, 8, 128...]
  transfers between devices with their start and end apart: 12 -> 0, of which waited for: 6 -> 0; matrix products, arithmetic and copies ran while one was open for 0% -> 0% of each run, Pallas kernels for 1% -> 0%
where the time goes in v2:
time: 120 us; the launch traced here: 119 us
  Pallas kernels  114 us (95%)
  local copies, waits for them, and re-layouts  4.17 us (3%)
    pallas_call x1, Pallas kernels, front(): pl.pallas_call(front_kernel, out_shape=[jax.ShapeDtypeStruct((128, 8, 128...  86.2 us
    pallas_call x1, Pallas kernels, dense(): pl.pallas_call(dense_kernel, out_shape=[jax.ShapeDtypeStruct((1152, 128),...  28.3 us
    unnamed x15, local copies, waits for them, and re-layouts  4.07 us

profile of v2, /device:TPU:1, one launch (start us, length us, event | category | flops | bytes accessed | tf_op | source)
XLA Modules:
  0.0 119.3 jit_solution(4536152403007822700)
XLA Ops:
  0.6 0.0 copy-start.5
  0.6 0.7 copy-done.5
  1.3 0.0 copy-start.6
  1.3 0.7 copy-done.6
  2.0 0.0 copy-start.2
  2.0 0.0 copy-start.3
  2.0 0.0 copy-start.4
  2.0 0.1 copy.9.ritz_ref
  2.1 0.6 copy-done.2
  2.7 0.0 copy-done.3
  2.7 0.0 copy-done.4
  2.7 0.0 copy-start
  2.7 1.1 copy-done
  3.7 0.0 copy-start.1
  3.8 1.1 copy-done.1
  4.8 86.2 %front.1 = (f32[128,8,128]{2,1,0:T(8,128)S(1)}, f32[96,1536]{1,0:T(8,128)S(1)}, f32[96,1536]{1,0:T(8,128)S(1)}, f32[96,1536]{1,0:T(8,128)S(1)}) custom-call(f32[1152,128]{1,0:T(8,128)S(1)} %bitcast.13, f32[1152,128]{1,0:T(8,128)S(1)} %bitcast.14, s32[4,128]{1,0:T(4,128)S(1)} %bitcast.16, s32[3,128]{1,0:T(4,128)S(1)} %bitcast.15, f32[24,24]{1,0:T(8,128)S(1)} %copy-done.2, ...), custom_call_target="tpu_custom_call" | custom-call | tf_op jit(solution)/shard_map/front/pallas_call | solution.py:534
  91.0 28.3 %dense.1 = (f32[1152,128]{1,0:T(8,128)}, f32[1152,128]{1,0:T(8,128)}) custom-call(f32[128,8,128]{2,1,0:T(8,128)S(1)} %get-tuple-element.8.gram_ref, f32[96,1536]{1,0:T(8,128)S(1)} %get-tuple-element.9.s_ref, f32[96,1536]{1,0:T(8,128)S(1)} %get-tuple-element.10.r_ref, f32[96,1536]{1,0:T(8,128)S(1)} %get-tuple-element.11.p_ref), custom_call_target="tpu_custom_call" | custom-call | tf_op jit(solution)/shard_map/dense/pallas_call | solution.py:584
  (1 shorter events, 0.0 us)
Async XLA Ops:
  0.6 0.7 copy-start.5
  1.3 0.7 copy-start.6
  2.0 0.7 copy-start.2
  2.0 0.7 copy-start.3
  2.0 0.7 copy-start.4
  2.7 1.1 copy-start
  3.7 1.1 copy-start.1

commit v3 on v2

--- a/solution.py
+++ b/solution.py
@@ -15,88 +15,103 @@
 BF16 = jnp.bfloat16
 VMEM = pl.BlockSpec(memory_space=pltpu.VMEM)
 SMEM = pl.BlockSpec(memory_space=pltpu.SMEM)
-ROOM = 48 * 2**20
+HBM = pl.BlockSpec(memory_space=pltpu.HBM)
+ROOM = 62 * 2**20
 UNKNOWNS = 196608
-UNROLL = 2
-COPIES = 38
-
-
-def mm(a, b):
-    return lax.dot_general(a, b, (((1,), (0,)), ((), ())), precision=HI, preferred_element_type=jnp.float32)
-
-def mm_t(a, b):
-    return lax.dot_general(a, b, (((0,), (0,)), ((), ())), precision=HI, preferred_element_type=jnp.float32)
-
-
-def sweep(block, factor):
+UNROLL = 12
+COPIES = 60
+PLANE = [(dx, dy) for dx in (2, 1, 3, 0) for dy in (2, 1, 3, 0) if (dx, dy) != (0, 0)]
+
+
+def sweep(block, factor=True):
     lane = lax.broadcasted_iota(jnp.int32, (8, 128), 1)
     sub = lax.broadcasted_iota(jnp.int32, (8, 128), 0)
     tiles = [block[8 * t : 8 * t + 8, :] for t in range(12)]
+
+    def spread(value, at):
+        return [jnp.broadcast_to(value[:, at + j : at + j + 1], (8, 128)) for j in range(4)]
+
+    def pick(column, at):
+        return jnp.broadcast_to(column[at : at + 1, :], (8, 128))
+
+    def square(at):
+        wide = spread(tiles[at // 8], at)
+        return [[pick(wide[j], at % 8 + i) if j >= i else None for j in range(4)] for i in range(4)]
+
     found = []
+    pivot = square(0)
     for group in range(24):
         p = 4 * group
         home, low = p // 8, p % 8
-        cols = [[jnp.broadcast_to(tile[:, p + j : p + j + 1], (8, 128)) for tile in tiles] for j in range(4)]
-        rows = [jnp.broadcast_to(tiles[home][low + j : low + j + 1, :], (8, 128)) for j in range(4)]
-
-        def entry(i, j):
-            return jnp.broadcast_to(cols[j][home][low + i : low + i + 1, :], (8, 128))
-
-        a00, a01, a11 = entry(0, 0), entry(0, 1), entry(1, 1)
-        b00, b01, b10, b11 = entry(0, 2), entry(0, 3), entry(1, 2), entry(1, 3)
-        c00, c01, c11 = entry(2, 2), entry(2, 3), entry(3, 3)
-        ia = 1.0 / (a00 * a11 - a01 * a01)
+        below = range(home if low == 0 else home + 1, 12)
+        cols = {t: spread(tiles[t], p) for t in below}
+        (a00, a01, b00, b01), (_, a11, b10, b11), (_, _, c00, c01), (_, _, _, c11) = pivot
+        ia = pl.reciprocal(a00 * a11 - a01 * a01)
         h00, h01, h11 = a11 * ia, -a01 * ia, a00 * ia
         x00, x01 = h00 * b00 + h01 * b10, h00 * b01 + h01 * b11
         x10, x11 = h01 * b00 + h11 * b10, h01 * b01 + h11 * b11
         s00 = c00 - (b00 * x00 + b10 * x10)
         s01 = c01 - (b00 * x01 + b10 * x11)
         s11 = c11 - (b01 * x01 + b11 * x11)
-        ic = 1.0 / (s00 * s11 - s01 * s01)
+        ic = pl.reciprocal(s00 * s11 - s01 * s01)
         g00, g01, g11 = s11 * ic, -s01 * ic, s00 * ic
+
+        def solve(f0, f1, f2, f3):
+            u0 = f2 - (x00 * f0 + x10 * f1)
+            u1 = f3 - (x01 * f0 + x11 * f1)
+            n2 = g00 * u0 + g01 * u1
+            n3 = g01 * u0 + g11 * u1
+            n0 = (h00 * f0 + h01 * f1) - (x00 * n2 + x01 * n3)
+            n1 = (h01 * f0 + h11 * f1) - (x10 * n2 + x11 * n3)
+            return [n0, n1, n2, n3], u0, u1
+
+        if group < 23:
+            q = p + 4
+            old = square(q)
+            ahead = [[pick(cols[q // 8][i], q % 8 + j) for i in range(4)] for j in range(4)]
+            factors = [solve(*ahead[j])[0] for j in range(4)]
+            pivot = [
+                [
+                    old[i][j]
+                    - ((ahead[i][0] * factors[j][0] + ahead[i][1] * factors[j][1])
+                       + (ahead[i][2] * factors[j][2] + ahead[i][3] * factors[j][3]))
+                    if j >= i else None
+                    for j in range(4)
+                ]
+                for i in range(4)
+            ]
         picked = (lane >= p) & (lane < p + 4)
-        full = [jnp.where(picked, jnp.where(lane == p + j, 1.0, 0.0), rows[j]) for j in range(4)]
-        u0 = full[2] - (x00 * full[0] + x10 * full[1])
-        u1 = full[3] - (x01 * full[0] + x11 * full[1])
-        n2 = g00 * u0 + g01 * u1
-        n3 = g01 * u0 + g11 * u1
-        v0 = h00 * full[0] + h01 * full[1]
-        v1 = h01 * full[0] + h11 * full[1]
-        n0 = v0 - (x00 * n2 + x01 * n3)
-        n1 = v1 - (x10 * n2 + x11 * n3)
-        new = [n0, n1, n2, n3]
-        if factor:
-            left = [jnp.where(lane < p + 4, f, 0.0) for f in full]
-            w0 = lax.rsqrt(a00)
-            l0 = left[0] * w0
-            e1 = a11 - a01 * a01 / a00
-            l1 = (left[1] - (a01 / a00) * left[0]) * lax.rsqrt(e1)
-            y0 = jnp.where(lane < p + 4, u0, 0.0)
-            y1 = jnp.where(lane < p + 4, u1, 0.0)
-            l2 = y0 * lax.rsqrt(s00)
-            l3 = (y1 - (s01 / s00) * y0) * lax.rsqrt(s11 - s01 * s01 / s00)
-            found.append([l0, l1, l2, l3])
-        fresh = []
-        for t, tile in enumerate(tiles):
-            kept = jnp.where(picked, 0.0, tile)
-            if t == home:
-                here = (sub >= low) & (sub < low + 4)
-                kept = jnp.where(here, 0.0, kept)
-                q = [jnp.where(here, jnp.where(sub == low + j, -1.0, 0.0), cols[j][t]) for j in range(4)]
-            else:
-                q = [cols[j][t] for j in range(4)]
-            fresh.append(kept - ((q[0] * n0 + q[1] * n1) + (q[2] * n2 + q[3] * n3)))
-        tiles = fresh
-    if factor:
-        out = []
-        for t in range(12):
-            eight = found[2 * t] + found[2 * t + 1]
-            tile = eight[0]
-            for s in range(1, 8):
-                tile = jnp.where(sub == s, eight[s], tile)
-            out.append(tile)
-        return jnp.concatenate(out, 0)
-    return jnp.concatenate(tiles, 0)
+        full = [jnp.where(picked, jnp.where(lane == p + j, 1.0, 0.0), pick(tiles[home], low + j)) for j in range(4)]
+        new, u0, u1 = solve(*full)
+        left = [jnp.where(lane < p + 4, f, 0.0) for f in full[:2]]
+        y0, y1 = (jnp.where(lane < p + 4, u, 0.0) for u in (u0, u1))
+        ra, rs = pl.reciprocal(a00), pl.reciprocal(s00)
+        e1, e3 = a11 - a01 * a01 * ra, s11 - s01 * s01 * rs
+        found.append(
+            [
+                left[0] * lax.rsqrt(a00),
+                (left[1] - a01 * ra * left[0]) * lax.rsqrt(e1),
+                y0 * lax.rsqrt(s00),
+                (y1 - s01 * rs * y0) * lax.rsqrt(e3),
+            ]
+        )
+        for t in below:
+            c = cols[t]
+            tiles[t] = jnp.where(picked, 0.0, tiles[t]) - (
+                (c[0] * new[0] + c[1] * new[1]) + (c[2] * new[2] + c[3] * new[3])
+            )
+    out = []
+    for t in range(12):
+        eight = found[2 * t] + found[2 * t + 1]
+        whole = eight[0]
+        for s in range(1, 8):
+            whole = jnp.where(sub == s, eight[s], whole)
+        out.append(whole)
+    return jnp.concatenate(out, 0)
+
+
+def mm(a, b):
+    return lax.dot_general(a, b, (((1,), (0,)), ((), ())), precision=HI, preferred_element_type=F32)
 
 
 def diagonal(block):
@@ -113,46 +128,42 @@
 
 
 def pad(block):
-    return jnp.concatenate([block, jnp.zeros((block.shape[0], 128 - block.shape[1]), jnp.float32)], 1)
-
-
-def rotation(gram, scale, rot_ref):
-    b = [gram[i] for i in range(6)]
-    a = [gram[6 + i] for i in range(6)]
+    return jnp.concatenate([block, jnp.zeros((block.shape[0], 128 - block.shape[1]), F32)], 1)
+
+
+def rotation(b, a, scale, rot_ref):
     m = [x + y for x, y in zip(a, b)]
-    d0, e0 = diagonal(m[0])
-    d1, e1 = diagonal(m[3])
-    d2, e2 = diagonal(m[5])
-    m11, m12, m13 = m[0] * d0 * e0, m[1] * d0 * e1, m[2] * d0 * e2
-    m22, m23, m33 = m[3] * d1 * e1, m[4] * d1 * e2, m[5] * d2 * e2
-    bsr_t, bsp_t, brp_t = (pad(cut(x).T) for x in (b[1], b[2], b[4]))
-    f1, f2, f3 = b[0] * d0, bsr_t * d1, bsp_t * d2
-    i1 = sweep(m11, False)
-    t1 = mm(cut(i1), jnp.concatenate([m12, m13, f1], 1))
-    t12, t13, y1 = t1[:, :128], t1[:, 128:256], t1[:, 256:]
-    s2 = jnp.concatenate([m22, m23, f2], 1) - mm(cut(m12).T, t1)
-    s3 = jnp.concatenate([m33, f3], 1) - mm(cut(m13).T, t1[:, 128:])
-    i2 = sweep(s2[:, :128], False)
-    m23 = s2[:, 128:256]
-    t2 = mm(cut(i2), s2[:, 128:])
-    s3 = s3 - mm(cut(m23).T, t2)
-    i3 = sweep(s3[:, :128], False)
-    w3 = mm(cut(i3), s3[:, 128:])
-    w2 = t2[:, 128:] - mm(cut(t2), w3)
-    w1 = y1 - mm(jnp.concatenate([cut(t12), cut(t13)], 1), jnp.concatenate([w2, w3], 0))
-    w = jnp.concatenate([w1 * d0, w2 * d1, w3 * d2], 0)
+    d1, e1 = diagonal(m[0])
+    d2, e2 = diagonal(m[3])
+    d3, e3 = diagonal(m[5])
+    b21, b31, b32 = (pad(cut(x).T) for x in (b[1], b[2], b[4]))
+    f1, f2, f3 = b[0] * d1, b21 * d2, b31 * d3
+    v1 = cut(sweep(m[0] * d1 * e1))
+    z1 = mm(v1, jnp.concatenate([m[1] * d1 * e2, m[2] * d1 * e3, f1], 1))
+    z12, z13, y1 = cut(z1), cut(z1[:, 128:]), z1[:, 256:]
+    s2 = jnp.concatenate([m[3] * d2 * e2, m[4] * d2 * e3, f2], 1) - mm(z12.T, z1)
+    s3 = jnp.concatenate([m[5] * d3 * e3, f3], 1) - mm(z13.T, z1[:, 128:])
+    v2 = cut(sweep(s2[:, :128]))
+    z2 = mm(v2, s2[:, 128:])
+    z23, y2 = cut(z2), z2[:, 128:]
+    s3 = s3 - mm(z23.T, z2)
+    v3 = cut(sweep(s3[:, :128]))
+    w3 = mm(v3.T, mm(v3, s3[:, 128:]))
+    w2 = mm(v2.T, y2 - mm(z23, w3))
+    w1 = mm(v1.T, y1 - mm(jnp.concatenate([z12, z13], 1), jnp.concatenate([w2, w3], 0)))
+    w = jnp.concatenate([w1 * d1, w2 * d2, w3 * d3], 0)
     big = jnp.concatenate(
         [
             jnp.concatenate([cut(b[0]), cut(b[1]), cut(b[2])], 1),
-            jnp.concatenate([cut(bsr_t), cut(b[3]), cut(b[4])], 1),
-            jnp.concatenate([cut(bsp_t), cut(brp_t), cut(b[5])], 1),
+            jnp.concatenate([cut(b21), cut(b[3]), cut(b[4])], 1),
+            jnp.concatenate([cut(b31), cut(b32), cut(b[5])], 1),
         ],
         0,
     )
     wt = cut(w).T
     small = mm(wt, mm(big, w))
     ds, es = diagonal(small)
-    inv = sweep(small * ds * es, True) * es
+    inv = sweep(small * ds * es) * es
     rot_ref[...] = mm(cut(inv), wt) * scale
 
 
@@ -324,14 +335,15 @@
 
 
 def front_kernel(
-    start_hbm, search_hbm, held_ref, ids_ref, kmat_ref, ritz_ref, moduli_ref,
-    gram_ref, s_out, r_out, p_out,
-    start_in, search_in, stencil_ref, s, r, p, image_s, columns, image, wide, blocks,
+    start_hbm, search_hbm, held_hbm, ids_hbm, kmat_hbm, ritz_hbm, moduli_hbm,
+    gram_ref, s_hbm, r_hbm, p_hbm,
+    s_out, r_out, p_out,
+    start_in, search_in, held_ref, ids_ref, kmat_ref, ritz_row, moduli_ref, ritz_ref, stencil_ref, s, r, p, image_s, columns, image, wide, blocks,
     s_pack, p_pack, r_pack, s_came, p_came, r_came,
     s_layer, r_layer, p_layer, s_edge, r_edge, p_edge,
     s_ahead, r_ahead, p_ahead, s_side, r_side, p_side, s_corner, r_corner, p_corner,
     back, back_over, back_corner, back_came, over_came, corner_came,
-    whole, g, from_core, half, from_x, quarter, from_y, from_z,
+    whole, g, from_core, half, from_plane, from_z,
     local, send, recv,
 ):
     axial, hoop = lax.axis_index("axial"), lax.axis_index("hoop")
@@ -349,15 +361,15 @@
 
     peers = {
         "core": [at(z, x, y, 1 - core)],
-        "x": [at(z, (x + d) % 4, y, core) for d in (1, 2, 3)],
-        "y": [at(z, x, (y + d) % 4, core) for d in (1, 2, 3)],
+        "plane": [at(z, (x + dx) % 4, (y + dy) % 4, core) for dx, dy in PLANE],
         "z": [at((z + d) % 4, x, y, core) for d in (1, 2, 3)],
         "hoop": [around(0, 1), around(0, -1), around(1, 1), around(-1, -1)],
     }
-    loads = [
-        pltpu.make_async_copy(start_hbm, start_in, local.at[0]),
-        pltpu.make_async_copy(search_hbm, search_in, local.at[1]),
-    ]
+    pairs = (
+        (start_hbm, start_in), (search_hbm, search_in), (held_hbm, held_ref), (ids_hbm, ids_ref),
+        (kmat_hbm, kmat_ref), (ritz_hbm, ritz_row), (moduli_hbm, moduli_ref),
+    )
+    loads = [pltpu.make_async_copy(source, target, local.at[n]) for n, (source, target) in enumerate(pairs)]
     for load in loads:
         load.start()
     barrier = pltpu.get_barrier_semaphore()
@@ -384,8 +396,8 @@
 
     def exchange(pack_ref, came_ref):
         copies = []
-        for d in (1, 2, 3):
-            copies.append(copy(pack_ref.at[(x + d) % 4], came_ref.at[x], peers["x"][d - 1]))
+        for d in (2, 1, 3):
+            copies.append(copy(pack_ref.at[(x + d) % 4], came_ref.at[x], at(z, (x + d) % 4, y, core)))
         return copies
 
     def forward(layer, edge, ahead, side, corner):
@@ -395,22 +407,29 @@
             copy(edge, corner, around(-1, -1)),
         ]
 
-    ids = ids_ref[...]
-    coef = jnp.zeros(ids.shape, F32)
-    for material in range(3):
-        coef = coef + jnp.where(ids == material, moduli_ref[material], 0.0)
-    free = (1 - held_ref[...]).astype(F32)
+    for load in loads[2:]:
+        load.wait()
+    coef = []
+    for layer in range(3):
+        ids = ids_ref[layer]
+        total = jnp.zeros((1, 128), F32)
+        for material in range(3):
+            total = total + jnp.where(ids == material, moduli_ref[0:1, material : material + 1], 0.0)
+        coef.append(total)
+    free = [(1 - held_ref[node]).astype(F32) for node in range(4)]
+    ritz = jnp.broadcast_to(jnp.concatenate([ritz_row[...], jnp.zeros((1, 32), F32)], 1), (K, 128))
+    ritz_ref[...] = jnp.sum(jnp.where(lane == lax.broadcasted_iota(jnp.int32, (K, 128), 0), ritz, 0.0), 1, keepdims=True)
     row = lax.broadcasted_iota(jnp.int32, (8, 128), 0)
     notes = []
     for node in range(4):
-        note = jnp.where(row == 0, free[node : node + 1], 0.0)
-        notes.append(jnp.where(row == 1, coef[node : node + 1], note) if node < 3 else note)
+        note = jnp.where(row == 0, free[node], 0.0)
+        notes.append(jnp.where(row == 1, coef[node], note) if node < 3 else note)
     for to, value in enumerate(swap(notes)):
         s_pack[to, 288:296, :] = value
 
     def mask_in(source, field_out):
         for i in range(12):
-            set_tile(field_out, i, source[pl.ds(i, K, stride=12), :] * free[i % 4 : i % 4 + 1])
+            set_tile(field_out, i, source[pl.ds(i, K, stride=12), :] * free[i % 4])
 
     loads[0].wait()
     mask_in(start_in, s_out)
@@ -426,6 +445,14 @@
     loads[1].wait()
     mask_in(search_in, p_out)
     pack(p_out, p_pack)
+    p_flying = exchange(p_pack, p_came)
+    p_came[x] = p_pack[x]
+    stores = [
+        pltpu.make_async_copy(s_out, s_hbm, local.at[7]),
+        pltpu.make_async_copy(p_out, p_hbm, local.at[8]),
+    ]
+    for store in stores:
+        store.start()
     finish(flying)
 
     unpack(s_came, s)
@@ -434,8 +461,6 @@
     coef = jnp.concatenate([note[1:2] for note in notes[:3]], 0)
     first_nodes(s, s_layer, s_edge)
     flying = forward(s_layer, s_edge, s_ahead, s_side, s_corner)
-    p_flying = exchange(p_pack, p_came)
-    p_came[x] = p_pack[x]
 
     def keep(index, value):
         blocks[index, :, 0:K] = value
@@ -460,8 +485,8 @@
     unpack(p_came, p)
     first_nodes(p, p_layer, p_edge)
     p_flying = forward(p_layer, p_edge, p_ahead, p_side, p_corner)
-    keep(2, mm_nt(s[...], p[...]))
-    keep(5, mm_nt(p[...], p[...]))
+    keep(1, mm_nt(s[...], p[...]))
+    keep(3, mm_nt(p[...], p[...]))
     finish(flying)
 
     over = over_came[...] + jnp.where(bottom, 0.0, jnp.where(lane < 32, turn(corner_came[...], 32), 0.0))
@@ -489,16 +514,17 @@
     products(columns, image, stencil_ref, coef)
     take(image, wide)
     p_ext = ext(p, p_ahead, p_side, corner)
-    keep(11, mm_nt(wide[...], p_ext))
-    for index, left, right in ((6, image_s, s), (7, image_s, r), (8, image_s, p), (1, s, r), (3, r, r), (4, r, p)):
+    keep(9, mm_nt(wide[...], p_ext))
+    for index, left, right in ((6, image_s, s), (7, image_s, p), (8, image_s, r), (2, s, r), (5, r, r), (4, p, r)):
         keep(index, mm_nt(left[...], right[...]))
     finish(flying)
     corner, far_edge = far_edges(r_side[...], r_corner[...], top)
     put(columns, r, r_ahead, r_side[...], far_edge, top)
     products(columns, image, stencil_ref, coef)
     take(image, wide)
-    keep(9, mm_nt(wide[...], ext(r, r_ahead, r_side, corner)))
-    keep(10, mm_nt(wide[...], ext(p, p_ahead, p_side, far_edges(p_side[...], p_corner[...], top)[0])))
+    keep(11, mm_nt(wide[...], ext(r, r_ahead, r_side, corner)))
+    p_ext = ext(p, p_ahead, p_side, far_edges(p_side[...], p_corner[...], top)[0])
+    keep(10, mm_nt(p_ext, wide[...]))
 
     for group in range(3):
         extra = jnp.where(lane < K, blocks[9 + group], 0.0)
@@ -510,19 +536,28 @@
 
     finish([copy(g.at[pl.ds((1 - core) * 64, 64)], from_core, peers["core"][0])])
     half[...] = g[pl.ds(core * 64, 64)] + from_core[...]
-    finish([copy(half.at[pl.ds((x + d) % 4 * 16, 16)], from_x.at[d - 1], peers["x"][d - 1]) for d in (1, 2, 3)])
-    quarter[...] = (half[pl.ds(x * 16, 16)] + from_x[0]) + (from_x[1] + from_x[2])
-    finish([copy(quarter.at[pl.ds((y + d) % 4 * 4, 4)], from_y.at[d - 1], peers["y"][d - 1]) for d in (1, 2, 3)])
-    from_z[z] = (quarter[pl.ds(y * 4, 4)] + from_y[0]) + (from_y[1] + from_y[2])
+    copies = []
+    for n, ((dx, dy), peer) in enumerate(zip(PLANE, peers["plane"])):
+        part = ((x + dx) % 4 * 4 + (y + dy) % 4) * 4
+        copies.append(copy(half.at[pl.ds(part, 4)], from_plane.at[n], peer))
+    finish(copies)
+    parts = [half[pl.ds((x * 4 + y) * 4, 4)]] + [from_plane[n] for n in range(15)]
+    while len(parts) > 1:
+        parts = [parts[n] + parts[n + 1] for n in range(0, len(parts), 2)]
+    from_z[z] = parts[0]
     finish([copy(from_z.at[z], from_z.at[z], peer) for peer in peers["z"]])
-    base = core * 64 + x * 16 + y * 4
+    base = core * 64 + (x * 4 + y) * 4
     whole[pl.ds(base, 4)] = (from_z[0] + from_z[1]) + (from_z[2] + from_z[3])
-    for axis, first, size in (("y", base, 4), ("x", core * 64 + x * 16, 16), ("core", core * 64, 64)):
+    for axis, first, size in (("plane", base, 4), ("core", core * 64, 64)):
         part = whole.at[pl.ds(first, size)]
         finish([copy(part, part, peer) for peer in peers[axis]])
     gram_ref[...] = whole[...]
     finish(r_flying)
     unpack(r_came, r_out)
+    stores.append(pltpu.make_async_copy(r_out, r_hbm, local.at[9]))
+    stores[2].start()
+    for store in stores:
+        store.wait()
 
 
 def front(start, search, held, ids, kmat, ritz, moduli):
@@ -530,13 +565,15 @@
         return pltpu.VMEM(shape + (128,), F32)
 
     field = pltpu.VMEM((K, 1536), F32)
-    anywhere = pl.BlockSpec(memory_space=pl.ANY)
     return pl.pallas_call(
         front_kernel,
         out_shape=[jax.ShapeDtypeStruct((128, 8, 128), F32)] + [jax.ShapeDtypeStruct((K, 1536), F32)] * 3,
-        in_specs=[anywhere] * 2 + [VMEM] * 4 + [SMEM],
-        out_specs=[VMEM] * 4,
-        scratch_shapes=[rows(1152)] * 2
+        in_specs=[HBM] * 7,
+        out_specs=[VMEM] + [HBM] * 3,
+        scratch_shapes=[field] * 3
+        + [rows(1152)] * 2
+        + [pltpu.VMEM((n, 1, 128), jnp.int32) for n in (4, 3)]
+        + [pltpu.VMEM(shape, F32) for shape in ((24, 24), (1, K), (1, 3), (K, 1))]
         + [pltpu.VMEM((96, 384), BF16)]
         + [field] * 4
         + [rows(K * 64)] * 2
@@ -546,8 +583,8 @@
         + [rows(288)] * 3 + [rows(K)] * 6
         + [rows(288), rows(K), rows(K)] * 2
         + [rows(n, 8) for n in (128, 128, 64, 64)]
-        + [rows(3, 16, 8), rows(16, 8), rows(3, 4, 8), rows(4, 4, 8)]
-        + [pltpu.SemaphoreType.DMA((2,)), pltpu.SemaphoreType.DMA((COPIES,)), pltpu.SemaphoreType.DMA((COPIES,))],
+        + [rows(15, 4, 8), rows(4, 4, 8)]
+        + [pltpu.SemaphoreType.DMA((10,)), pltpu.SemaphoreType.DMA((COPIES,)), pltpu.SemaphoreType.DMA((COPIES,))],
         compiler_params=pltpu.CompilerParams(vmem_limit_bytes=ROOM, collective_id=0, has_side_effects=True),
         name="front",
     )(start, search, held, ids, kmat, ritz, moduli)
@@ -568,12 +605,21 @@
     return blocks
 
 
-def dense_kernel(gram_ref, s_ref, r_ref, p_ref, block_ref, search_ref, rot_ref):
-    rotation(unpack_gram(gram_ref), math.sqrt(UNKNOWNS), rot_ref)
+def dense_kernel(gram_ref, s_hbm, r_hbm, p_hbm, block_ref, search_ref, rot_ref, s_ref, r_ref, p_ref, local):
+    loads = [
+        pltpu.make_async_copy(source, target, local.at[n])
+        for n, (source, target) in enumerate(((s_hbm, s_ref), (r_hbm, r_ref), (p_hbm, p_ref)))
+    ]
+    for load in loads:
+        load.start()
+    blocks = unpack_gram(gram_ref)
+    rotation(blocks[:6], blocks[6:], math.sqrt(UNKNOWNS), rot_ref)
     rot = rot_ref[...]
+    for load in loads:
+        load.wait()
     for i in range(6):
         lanes = slice(256 * i, 256 * i + 256)
-        tail = mm(rot[:, K:], jnp.concatenate([r_ref[:, lanes], p_ref[:, lanes]], 0))
+        tail = mm(rot[:, K:], jnp.concatenate([p_ref[:, lanes], r_ref[:, lanes]], 0))
         head = tail + mm(rot[:, :K], s_ref[:, lanes])
         for h in range(2):
             block_ref[pl.ds(2 * i + h, K, stride=12), :] = head[:, 128 * h : 128 * h + 128]
@@ -584,9 +630,9 @@
     return pl.pallas_call(
         dense_kernel,
         out_shape=[jax.ShapeDtypeStruct((1152, 128), F32)] * 2,
-        in_specs=[VMEM] * 4,
+        in_specs=[VMEM] + [HBM] * 3,
         out_specs=[VMEM] * 2,
-        scratch_shapes=[pltpu.VMEM((K, 288), F32)],
+        scratch_shapes=[pltpu.VMEM((K, 288), F32)] + [pltpu.VMEM((K, 1536), F32)] * 3 + [pltpu.SemaphoreType.DMA((3,))],
         compiler_params=pltpu.CompilerParams(vmem_limit_bytes=ROOM),
         name="dense",
     )(gram, s, r, p)
@@ -595,8 +641,8 @@
 def on_device(start_block, search_block, ritz_values, element_matrix, moduli, material_ids, held):
     shape = start_block.shape
     gram, s, r, p = front(
-        start_block.reshape(1152, 128), search_block.reshape(1152, 128), held.reshape(4, 128),
-        material_ids.reshape(3, 128), element_matrix, ritz_values.reshape(K, 1), moduli,
+        start_block.reshape(1152, 128), search_block.reshape(1152, 128), held,
+        material_ids, element_matrix, ritz_values.reshape(1, K), moduli.reshape(1, 3),
     )
     block, search = dense(gram, s, r, p)
     return block.reshape(shape), search.reshape(shape)

time: 120 us -> 95.5 us (0.80)
  Pallas kernels: 114 us -> 94.4 us
  local copies, waits for them, and re-layouts: 4.17 us -> 0 us
    pallas_call x1, Pallas kernels: 86.2 us -> 73.2 us  [front(): pl.pallas_call(front_kernel, out_shape=[jax.ShapeDtypeStruct((128, 8, 128...]
    pallas_call x1, Pallas kernels: 28.3 us -> 21.3 us  [dense(): pl.pallas_call(dense_kernel, out_shape=[jax.ShapeDtypeStruct((1152, 128),...]
    unnamed x15 -> x0, local copies, waits for them, and re-layouts: 4.07 us -> none
where the time goes in v3:
time: 95.5 us; the launch traced here: 95.3 us
  Pallas kernels  94.4 us (99%)
    pallas_call x1, Pallas kernels, front(): pl.pallas_call(front_kernel, out_shape=[jax.ShapeDtypeStruct((128, 8, 128...  73.2 us
    pallas_call x1, Pallas kernels, dense(): pl.pallas_call(dense_kernel, out_shape=[jax.ShapeDtypeStruct((1152, 128),...  21.3 us

profile of v3, /device:TPU:1, one launch (start us, length us, event | category | flops | bytes accessed | tf_op | source)
XLA Modules:
  0.0 95.3 jit_solution(10909121491150057664)
XLA Ops:
  0.6 73.2 %front.1 = (f32[128,8,128]{2,1,0:T(8,128)}, f32[96,1536]{1,0:T(8,128)}, f32[96,1536]{1,0:T(8,128)}, f32[96,1536]{1,0:T(8,128)}) custom-call(f32[1152,128]{1,0:T(8,128)} %bitcast.10, f32[1152,128]{1,0:T(8,128)} %bitcast.11, s32[4,1,128]{2,1,0:T(1,128)} %held_hbm.1, s32[3,1,128]{2,1,0:T(1,128)} %ids_hbm.1, f32[24,24]{1,0:T(8,128)} %kmat_hbm.1, ...), custom_call_target="tpu_custom_call" | custom-call | tf_op jit(solution)/shard_map/front/pallas_call | solution.py:568
  73.8 21.3 %dense.1 = (f32[1152,128]{1,0:T(8,128)}, f32[1152,128]{1,0:T(8,128)}) custom-call(f32[128,8,128]{2,1,0:T(8,128)} %get-tuple-element.8.gram_ref, f32[96,1536]{1,0:T(8,128)} %get-tuple-element.9.s_hbm, f32[96,1536]{1,0:T(8,128)} %get-tuple-element.10.r_hbm, f32[96,1536]{1,0:T(8,128)} %get-tuple-element.11.p_hbm), custom_call_target="tpu_custom_call" | custom-call | tf_op jit(solution)/shard_map/dense/pallas_call | solution.py:630
